TPU v7x, 32 devices: a whole 2x2x4 slice. The times are simulated.
32 devices in a mesh: seq: 32 (over z, y, x, core), head: 1.
Axes of the slice: x: 2, y: 2, z: 4, core: 2. Of those that a mesh axis runs over, the one named last changes fastest.
Arguments:
- video: bfloat16 [8192, 3072], P('seq'), may hold values from -6 to 6
- cotangent: bfloat16 [8192, 3072], P('seq'), may hold values from -48 to 48
- text_embed: bfloat16 [256, 4096], P(None, 'seq'), may hold values from -700 to 700
- text_gain: float32 [4096], P('seq'), may hold values from 0.25 to 1.75
- w_query: bfloat16 [3072, 3072], P('seq', 'head'), may hold values from -0.109375 to 0.109375
- w_key: bfloat16 [4096, 3072], P('seq', 'head'), may hold values from -0.09375 to 0.09375
- w_value: bfloat16 [4096, 3072], P('seq', 'head'), may hold values from -0.09375 to 0.09375
- w_out: bfloat16 [3072, 3072], P('head', 'seq'), may hold values from -0.109375 to 0.109375
Outputs:
- grad_video: bfloat16 [8192, 3072], P('seq', 'head')
- grad_text: float32 [256, 4096], P(None, 'seq')
All inputs are finite; a program needn't handle non-finite values.
Results may differ from a plain program's by a relative error of at most 0.012.
Values may be sent and summed in bfloat16 or wider, within the bound.
A program may use at most 128 MiB of HBM per device.

v0:
```python
import jax
import jax.numpy as jnp
from jax import lax
from jax.sharding import PartitionSpec as P

HEAD_DIM = 128
TEXT_DIM = 4096


epsilon = 1e-06


def body(video, cotangent, text_embed, text_gain, w_query, w_key, w_value, w_out):
    contract = (((1,), (1,)), ((), ()))
    tok_rows = video.shape[0]
    text_rows = text_embed.shape[0]
    local_width = w_key.shape[1]
    local_heads = local_width // HEAD_DIM
    score_scale = HEAD_DIM ** (-0.5)
    text_wide = text_embed.astype(jnp.float32)
    scaled_text = (text_wide * text_gain).astype(jnp.bfloat16)
    key_part = jnp.dot(scaled_text, w_key, preferred_element_type=jnp.float32)
    value_part = jnp.dot(scaled_text, w_value, preferred_element_type=jnp.float32)
    square_part = jnp.sum(text_wide * text_wide, axis=1)
    key_sum, value_sum, square_sum = lax.psum((key_part, value_part, square_part), "seq")
    inverse_rms = lax.rsqrt(square_sum / TEXT_DIM + epsilon)[:, None]
    keys = (inverse_rms * key_sum).astype(jnp.bfloat16)
    text_values = (inverse_rms * value_sum).astype(jnp.bfloat16)
    full_query = lax.all_gather(w_query, "seq", axis=0, tiled=True)
    query = jnp.dot(video, full_query, preferred_element_type=jnp.float32).astype(jnp.bfloat16)
    grad_out = lax.dot_general(
        cotangent,
        lax.all_gather(w_out, "seq", axis=1, tiled=True),
        contract,
        preferred_element_type=jnp.float32,
    ).astype(jnp.bfloat16)
    query_heads = query.reshape(tok_rows, local_heads, HEAD_DIM)
    grad_heads = grad_out.reshape(tok_rows, local_heads, HEAD_DIM)
    key_heads = keys.reshape(text_rows, local_heads, HEAD_DIM)
    value_heads = text_values.reshape(text_rows, local_heads, HEAD_DIM)
    scores = (
        jnp.einsum("thd,lhd->htl", query_heads, key_heads, preferred_element_type=jnp.float32)
        * score_scale
    )
    raised = jnp.exp(scores)
    softmax_out = raised / jnp.sum(raised, axis=2, keepdims=True)
    grad_probs = jnp.einsum(
        "thd,lhd->htl", grad_heads, value_heads, preferred_element_type=jnp.float32
    )
    row_delta = jnp.sum(grad_probs * softmax_out, axis=2, keepdims=True)
    grad_scores = (softmax_out * (grad_probs - row_delta) * score_scale).astype(jnp.bfloat16)
    grad_query = (
        jnp.einsum("htl,lhd->thd", grad_scores, key_heads, preferred_element_type=jnp.float32)
        .astype(jnp.bfloat16)
        .reshape(tok_rows, local_width)
    )
    grad_key_part = jnp.einsum(
        "htl,thd->lhd", grad_scores, query_heads, preferred_element_type=jnp.float32
    ).reshape(text_rows, local_width)
    grad_value_part = jnp.einsum(
        "htl,thd->lhd",
        softmax_out.astype(jnp.bfloat16),
        grad_heads,
        preferred_element_type=jnp.float32,
    ).reshape(text_rows, local_width)
    grad_keys, grad_values = lax.psum((grad_key_part, grad_value_part), "seq")
    normed_part = lax.dot_general(
        grad_keys.astype(jnp.bfloat16), w_key, contract, preferred_element_type=jnp.float32
    ) + lax.dot_general(
        grad_values.astype(jnp.bfloat16), w_value, contract, preferred_element_type=jnp.float32
    )
    grad_normed = lax.psum(normed_part.astype(jnp.bfloat16), "head").astype(jnp.float32)
    normed = text_wide * inverse_rms
    row_stat = lax.psum(jnp.sum(grad_normed * text_gain * normed, axis=1), "seq")
    grad_text = inverse_rms * (grad_normed * text_gain - normed * (row_stat / TEXT_DIM)[:, None])
    video_terms = lax.dot_general(
        grad_query,
        lax.all_gather(w_query, "seq", axis=0, tiled=True),
        contract,
        preferred_element_type=jnp.float32,
    )
    grad_video = lax.psum_scatter(
        video_terms.astype(jnp.bfloat16), "head", scatter_dimension=1, tiled=True
    )
    return (grad_video, grad_text)


def solution(mesh):
    in_specs = (
        P("seq", None),
        P("seq", None),
        P(None, "seq"),
        P("seq"),
        P("seq", "head"),
        P("seq", "head"),
        P("seq", "head"),
        P("head", "seq"),
    )
    out_specs = (P("seq", "head"), P(None, "seq"))
    return jax.shard_map(body, mesh=mesh, in_specs=in_specs, out_specs=out_specs, check_vma=False)
```

profile of v0, /device:TPU:4, one launch (start us, length us, event | category | flops | bytes accessed | tf_op | source)
XLA Modules:
  0.0 655.0 jit_solution(5861853452150477)
XLA Ops:
  7.2 0.0 copy-start
  7.2 0.0 copy-start.10
  7.2 0.0 copy-start.7
  7.2 0.0 all-reduce.5.cloned.1.call-start
  7.3 1.1 copy.10
  8.3 3.5 fusion.48
  11.9 0.0 copy-done.10
  11.9 0.0 copy-done.7
  11.9 2.3 fusion.46
  14.2 0.0 all-reduce.5.cloned.1.call-update
  14.2 0.0 all-gather.5.cloned.1.call-start
  14.3 0.7 all-gather.5.cloned.1.call-update
  15.0 0.0 all-gather.3.cloned.1.call-start
  15.0 0.7 all-gather.3.cloned.1.call-update
  15.7 43.0 %psum.45 = f32[256]{0:T(256)S(1)} all-reduce(f32[256]{0:T(256)S(1)} %fusion.44), channel_id=1, replica_groups=mesh['seq'=32,'head'=1] {'seq'}, use_global_device_ids=true, to_apply=%region_1.0 | all-reduce | flops 256 | bytes 2048 | tf_op jit(solution)/shard_map/psum | solution.py:25
  58.7 113.8 %all-reduce.5.cloned.1.call-done = (f32[256,3072]{1,0:T(8,128)}, f32[256,3072]{1,0:T(8,128)}) async-done(((f32[256,3072]{1,0:T(8,128)}, f32[256,3072]{1,0:T(8,128)}), (f32[256,3072]{1,0:T(8,128)}, f32[256,3072]{1,0:T(8,128)})) %all-reduce.5.cloned.1.call-update) | async-done | bytes 6291472 | tf_op jit(solution)/shard_map/psum | solution.py:25
  172.6 4.8 fusion.19
  177.4 2.6 copy.25
  180.0 120.5 %all-gather.5.cloned.1.call-done = bf16[3072,3072]{0,1:T(8,128)(2,1)} async-done(((bf16[3072,96]{0,1:T(8,128)(2,1)}), bf16[3072,3072]{0,1:T(8,128)(2,1)}) %all-gather.5.cloned.1.call-update) | async-done | bytes 18874384 | tf_op jit(solution)/shard_map/all_gather | solution.py:33
  300.6 0.0 copy-done
  300.6 10.4 %convolution_convert_fusion.1 = bf16[256,3072]{1,0:T(8,128)(2,1)} fusion(bf16[256,3072]{1,0:T(8,128)(2,1)S(1)} %copy-done, bf16[3072,3072]{0,1:T(8,128)(2,1)} %all-gather.5.cloned.1.call-done), kind=kOutput, calls=%fused_computation.8 | convolution fusion | flops 4832624640 | bytes 22020096 | tf_op jit(solution)/shard_map/dot_general | solution.py:31
  310.9 1.7 copy.27
  312.7 114.1 %all-gather.3.cloned.1.call-done = bf16[3072,3072]{1,0:T(8,128)(2,1)} async-done(((bf16[96,3072]{1,0:T(8,128)(2,1)}), bf16[3072,3072]{1,0:T(8,128)(2,1)}) %all-gather.3.cloned.1.call-update) | async-done | bytes 18874384 | tf_op jit(solution)/shard_map/all_gather | solution.py:29
  426.8 10.3 %convolution_convert_fusion.2 = bf16[256,3072]{1,0:T(8,128)(2,1)} fusion(bf16[256,3072]{1,0:T(8,128)(2,1)} %param.8, bf16[3072,3072]{1,0:T(8,128)(2,1)} %all-gather.3.cloned.1.call-done), kind=kOutput, calls=%fused_computation.9 | convolution fusion | flops 4832624640 | bytes 22020096 | tf_op jit(solution)/shard_map/dot_general | solution.py:30
  437.1 2.6 copy.26
  439.6 0.0 copy-start.3
  439.6 0.0 copy-start.5
  439.6 3.6 fusion.20
  443.2 0.0 copy-done.3
  443.2 0.0 copy-done.5
  443.2 1.3 fusion.3
  444.6 0.0 copy-start.2
  444.6 2.7 copy-done.2
  447.3 0.0 copy-start.4
  447.3 3.0 fusion.12
  450.2 0.0 copy-done.4
  450.2 0.0 copy-start.6
  450.2 12.5 %fusion.16 = bf16[24,128,256]{2,1,0:T(8,128)(2,1)} fusion(bf16[256,24,128]{0,2,1:T(8,128)(2,1)S(1)} %bitcast.38, f32[24,256,256]{1,2,0:T(8,128)} %fusion.20, f32[24,256,256]{1,2,0:T(8,128)} %copy-done.2, f32[24,256]{1,0:T(8,128)S(1)} %get-tuple-element.10), kind=kOutput, calls=%fused_computation.18 | convolution fusion | flops 417601792 | bytes 15753216 | tf_op jit(solution)/shard_map/htl,lhd->thd/dot_general | solution.py:53
  462.7 0.0 copy-done.6
  462.7 13.0 %fusion.7 = f32[24,128,256]{2,1,0:T(8,128)} fusion(bf16[256,24,128]{0,2,1:T(8,128)(2,1)S(1)} %bitcast.40, f32[24,256,256]{1,2,0:T(8,128)} %fusion.20, f32[24,256,256]{1,2,0:T(8,128)} %copy-done.2, f32[24,256]{1,0:T(8,128)S(1)} %get-tuple-element.10), kind=kOutput, calls=%fused_computation.10 | convolution fusion | flops 416815360 | bytes 17326080 | tf_op jit(solution)/shard_map/htl,thd->lhd/dot_general | solution.py:57
  475.7 0.0 copy-start.8
  475.7 0.0 copy-start.9
  475.7 119.2 %all-reduce.6 = (bf16[256,3072]{0,1:T(8,128)(2,1)}, bf16[256,3072]{0,1:T(8,128)(2,1)S(1)}) all-reduce(f32[256,3072]{0,1:T(8,128)} %bitcast.41, f32[256,3072]{0,1:T(8,128)} %bitcast.42), channel_id=1, replica_groups=mesh['seq'=32,'head'=1] {'seq'}, use_global_device_ids=true, to_apply=%region_7.0 | all-reduce | flops 1572864 | bytes 9437184 | tf_op jit(solution)/shard_map/psum | solution.py:66
  594.9 0.0 copy-done.8
  594.9 1.8 fusion.59
  596.7 0.0 copy-done.9
  596.7 0.4 fusion.41
  597.1 40.0 %psum.50 = f32[256]{0:T(256)S(1)} all-reduce(f32[256]{0:T(256)S(1)} %get-tuple-element.12), channel_id=1, replica_groups=mesh['seq'=32,'head'=1] {'seq'}, use_global_device_ids=true, to_apply=%region_9.0 | all-reduce | flops 256 | bytes 2048 | tf_op jit(solution)/shard_map/psum | solution.py:74
  637.2 0.8 copy.21
  638.0 0.0 copy-start.1
  638.0 10.5 %convolution_convert_fusion = bf16[256,3072]{1,0:T(8,128)(2,1)} fusion(bf16[256,3072]{0,1:T(8,128)(2,1)} %bitcast.43, bf16[3072,3072]{1,0:T(8,128)(2,1)} %all-gather.3.cloned.1.call-done), kind=kOutput, calls=%fused_computation.7 | convolution fusion | flops 4832624640 | bytes 22020096 | tf_op jit(solution)/shard_map/dot_general | solution.py:76
  648.4 0.0 copy-done.1
  (4 shorter events, 0.1 us)
Async XLA Ops:
  7.2 293.4 %copy-start = (bf16[256,3072]{1,0:T(8,128)(2,1)S(1)}, bf16[256,3072]{1,0:T(8,128)(2,1)}, u32[]{:S(2)}) copy-start(bf16[256,3072]{1,0:T(8,128)(2,1)} %param.9) | copy-start | bytes 4718596
  7.2 4.7 copy-start.10
  7.2 4.7 copy-start.7
  7.2 165.4 %all-reduce.5.cloned.1.call-start = ((), (), s32[]{:S(2)}) async-start(), calls=%async_computation.2 | async-start | bytes 12582912 | tf_op jit(solution)/shard_map/psum | solution.py:25
  14.2 286.4 %all-gather.5.cloned.1.call-start = ((), (), s32[]{:S(2)}) async-start(), calls=%async_computation.1 | async-start | bytes 19464192 | tf_op jit(solution)/shard_map/all_gather | solution.py:33
  15.0 411.8 %all-gather.3.cloned.1.call-start = ((), (), s32[]{:S(2)}) async-start(), calls=%async_computation | async-start | bytes 19464192 | tf_op jit(solution)/shard_map/all_gather | solution.py:29
  439.6 3.6 copy-start.3
  439.6 3.6 copy-start.5
  444.6 2.7 copy-start.2
  447.3 3.0 copy-start.4
  450.2 12.5 %copy-start.6 = (bf16[256,3072]{0,1:T(8,128)(2,1)S(1)}, bf16[256,3072]{0,1:T(8,128)(2,1)}, u32[]{:S(2)}) copy-start(bf16[256,3072]{0,1:T(8,128)(2,1)} %copy.26) | copy-start | bytes 4718596
  475.7 119.2 %copy-start.8 = (bf16[128,3072]{1,0:T(8,128)(2,1)S(1)}, bf16[128,3072]{1,0:T(8,128)(2,1)}, u32[]{:S(2)}) copy-start(bf16[128,3072]{1,0:T(8,128)(2,1)} %param.14) | copy-start | bytes 2359300
  475.7 121.0 %copy-start.9 = (bf16[128,3072]{1,0:T(8,128)(2,1)S(1)}, bf16[128,3072]{1,0:T(8,128)(2,1)}, u32[]{:S(2)}) copy-start(bf16[128,3072]{1,0:T(8,128)(2,1)} %param.13) | copy-start | bytes 2359300
  638.0 10.5 %copy-start.1 = (bf16[256,3072]{1,0:T(8,128)(2,1)S(1)}, bf16[256,3072]{1,0:T(8,128)(2,1)}, u32[]{:S(2)}) copy-start(bf16[256,3072]{1,0:T(8,128)(2,1)} %param.9) | copy-start | bytes 4718596
Sparse Core Ops, SparseCore 0:
  14.3 158.2 all-reduce.4
  175.9 124.6 all-gather.4
  303.9 122.8 all-gather.2
where the time goes:
time: 656 us; the launch traced here: 655 us
  waiting for transfers between devices  350 us (53%)
  blocking collectives  202 us (31%)
  matrix products  72.5 us (11%)
  between operations  13.8 us (2%)
  local copies, waits for them, and re-layouts  11.5 us (2%)
    all_gather x1, waiting for transfers between devices, body(): lax.all_gather(w_out, 'seq', axis=1, tiled=True)  121 us
    psum x1, blocking collectives, body(): grad_keys, grad_values = lax.psum((grad_key_part, grad_value_part), 'seq')  119 us
    all_gather x1, waiting for transfers between devices, body(): full_query = lax.all_gather(w_query, 'seq', axis=0, tiled=True)  114 us
    psum x1, waiting for transfers between devices, body(): lax.psum((key_part, value_part, square_part), 'seq')  114 us
    psum x1, blocking collectives, body(): lax.psum((key_part, value_part, square_part), 'seq')  43 us
    psum x1, blocking collectives, body(): lax.psum(jnp.sum(grad_normed * text_gain * normed, axis=1), 'seq')  40 us
  transfers between devices with their start and end apart: 3, of which 3 were waited for; matrix products, arithmetic and copies ran while one was open for 3% of the time, Pallas kernels for 0%

commit v1 on v0

v1 whole, which is shorter than its diff:
```python
import functools
import math

import jax
import jax.numpy as jnp
from jax import lax
from jax.experimental import pallas as pl
from jax.experimental.pallas import tpu as pltpu
from jax.sharding import PartitionSpec as P

HEAD_DIM = 128
ROWS = 16
MESH = pl.DeviceIdType.MESH
epsilon = 1e-06
F32 = jnp.float32
BF16 = jnp.bfloat16


def dot(a, b, dims):
    return lax.dot_general(a, b, ((dims[0:1], dims[1:2]), ((), ())), preferred_element_type=F32)


def kernel(
    n, text_dim, scaled, squares, w_key, w_value, w_query, w_out, video, cotangent,
    grad_video, grad_normed, row_stat, inverse,
    wq, wo, vid, cot, wk, wv, st, sq, sq_in,
    sums, halves, keys, grads, ghalves, gfull, query, gout, gquery, gv_send, gv_recv, gv_own, tail_send, tail_recv,
    pair_send, pair_recv, local_sem, w_send, w_recv, sq_send, sq_recv, k_send, k_recv, g_send, g_recv, end_send, end_recv,
):
    me = lax.axis_index("seq")
    chip, core = me // 2, me % 2
    other = 1 - core
    sibling = me + 1 - 2 * core
    n_bits = int(math.log2(n // 2))
    bit = [(chip // (1 << b)) % 2 for b in range(n_bits)]
    partner = [me + (1 - 2 * bit[b]) * (2 << b) for b in range(n_bits)]
    low = list(range(min(2, n_bits)))
    high = list(range(2, n_bits))
    gather_order = [high + low, high + low[::-1]]
    reduce_order = [low + high, low[::-1] + high]
    width = wq.shape[2]
    toks = vid.shape[1]
    pending = []

    barrier = pltpu.get_barrier_semaphore()
    for peer in [sibling] + partner:
        pl.semaphore_signal(barrier, inc=1, device_id={"seq": peer}, device_id_type=MESH)
    pl.semaphore_wait(barrier, 1 + n_bits)

    def send(src, dst, send_sem, recv_sem, peer):
        copy = pltpu.make_async_remote_copy(
            src_ref=src, dst_ref=dst, send_sem=send_sem, recv_sem=recv_sem,
            device_id={"seq": peer}, device_id_type=MESH,
        )
        copy.start()
        pending.append(copy)
        return copy

    mine = pl.ds(pl.multiple_of(core * width, 128), width)
    theirs = pl.ds(pl.multiple_of(other * width, 128), width)
    plan = [
        (scaled, scaled, st.at[core]),
        (w_key.at[:, mine], w_key.at[:, theirs], wk.at[core]),
        (w_value.at[:, mine], w_value.at[:, theirs], wv.at[core]),
        (squares, squares, sq.at[core]),
        (w_query.at[:, mine], w_query.at[:, theirs], wq.at[me]),
        (w_out.at[:, mine], w_out.at[:, theirs], wo.at[me]),
        (video, video, vid.at[core]),
        (cotangent, cotangent, cot.at[core]),
    ]
    shared = []
    for i, (own, away, dst) in enumerate(plan):
        remote = send(away, dst, pair_send.at[i], pair_recv.at[i], sibling)
        local = pltpu.make_async_copy(own, dst, local_sem.at[i])
        local.start()
        shared.append((remote, local))

    def have(i):
        shared[i][0].wait_recv()
        shared[i][1].wait()

    arrivals = {}

    def weights(array, buffer, p):
        for stream in range(2):
            order = gather_order[stream]
            where = chip
            for t in range(n_bits):
                if (p >> t) & 1:
                    where = where + (1 - 2 * bit[order[t]]) * (1 << order[t])
            block = buffer.at[2 * where + stream]
            if p > 0:
                arrivals[array, stream, p].wait_recv()
            for t in range(p.bit_length(), n_bits):
                q = p + (1 << t)
                arrivals[array, stream, q] = send(
                    block, block, w_send.at[array, stream, q], w_recv.at[array, stream, q], partner[order[t]]
                )

    def reduce_gather(parts, landing, full, send_sem, recv_sem, finish):
        held = parts.shape[1]
        base = [0, 0]
        sizes, bases = [], []
        offset = 0
        for step in range(n_bits):
            half = max(held // 2, 1)
            sent = []
            for i in range(2):
                b = reduce_order[i][step]
                if held > 1:
                    away = base[i] + (1 - bit[b]) * half
                    base[i] = base[i] + bit[b] * half
                else:
                    away = base[i]
                sent.append(
                    send(
                        parts.at[i, pl.ds(away, half)], landing.at[i, pl.ds(offset, half)],
                        send_sem.at[i, step], recv_sem.at[i, step], partner[b],
                    )
                )
            yield
            for i in range(2):
                sent[i].wait_recv()
                if held == 1:
                    sent[i].wait_send()
                    pending[:] = [copy for copy in pending if copy is not sent[i]]
                spot = pl.ds(base[i], half)
                total = parts[i, spot].astype(F32) + landing[i, offset : offset + half].astype(F32)
                parts[i, spot] = total.astype(BF16)
            sizes.append((step, half) if held > 1 else None)
            bases.append(list(base))
            offset += half
            held = half
        for i in range(2):
            finish(i, base[i], held)
        for entry in range(n_bits - 1, -1, -1):
            if sizes[entry] is None:
                continue
            step, half = sizes[entry]
            sent = []
            for i in range(2):
                spot = full.at[i, pl.ds(bases[entry][i], half)]
                sent.append(
                    send(
                        spot, spot, send_sem.at[i, n_bits + step], recv_sem.at[i, n_bits + step],
                        partner[reduce_order[i][step]],
                    )
                )
            yield
            for i in range(2):
                sent[i].wait_recv()

    def square_sum():
        have(3)
        sq_in[0] = sq[0] + sq[1]
        for b in range(n_bits):
            copy = send(sq_in.at[b], sq.at[2 + b], sq_send.at[b], sq_recv.at[b], partner[b])
            yield
            copy.wait_recv()
            sq_in[b + 1] = sq_in[b] + sq[2 + b]
        inverse[...] = lax.rsqrt(sq_in[n_bits] / text_dim + epsilon)

    def drain(generator, steps=None):
        count = 0
        for _ in generator:
            count += 1
            if steps is not None and count >= steps:
                return

    pieces = sums.shape[1]
    for i in range(3):
        have(i)
    for i, w in ((0, wk), (1, wv)):
        part = dot(st[0], w[0], (1, 0)) + dot(st[1], w[1], (1, 0))
        sums[i] = part.astype(BF16).reshape(pieces, ROWS, width)

    def finish_keys(i, base, held):
        inv = inverse[pl.ds(pl.multiple_of(base * ROWS, ROWS), held * ROWS), :][:, 0:1]
        total = sums[i, pl.ds(base, held)].astype(F32).reshape(held * ROWS, width)
        keys[i, pl.ds(base, held)] = (inv * total).astype(BF16).reshape(held, ROWS, width)

    text_sum = reduce_gather(sums, halves, keys, k_send, k_recv, finish_keys)
    norm_sum = square_sum()
    next(text_sum)
    next(norm_sum)
    have(4)
    weights(0, wq, 0)
    have(5)
    weights(1, wo, 0)
    blocks = 1 << n_bits
    near = blocks // 2
    small = [(0, wq, p) for p in range(1, near)] + [(1, wo, p) for p in range(1, near)]
    for i, event in enumerate(small):
        weights(*event)
        drain(norm_sum, 1)
        if i >= 1:
            drain(text_sum, 1)
    drain(norm_sum)
    drain(text_sum)
    for p in range(near, blocks):
        weights(0, wq, p)
    have(6)
    tile = 256 if width % 256 == 0 else 128

    def project(rows, w, out):
        def body(t, _):
            cols = pl.ds(pl.multiple_of(t * tile, tile), tile)
            wide = w[:, :, cols].reshape(-1, tile)
            out[:, cols] = dot(rows[...].reshape(2 * toks, -1), wide, (1, 0)).astype(BF16)
            return 0

        lax.fori_loop(0, width // tile, body, 0)

    project(vid, wq, query)
    for p in range(near, blocks):
        weights(1, wo, p)
    have(7)
    project(cot, wo, gout)

    scale = HEAD_DIM ** (-0.5)
    text_len = pieces * ROWS

    def attention(h, _):
        cols = pl.ds(pl.multiple_of(h * HEAD_DIM, HEAD_DIM), HEAD_DIM)
        key = keys[0, :, :, cols].reshape(text_len, HEAD_DIM)
        value = keys[1, :, :, cols].reshape(text_len, HEAD_DIM)
        q, g = query[:, cols], gout[:, cols]
        raised = jnp.exp(dot(key, q, (1, 1)) * scale)
        probs = raised / jnp.sum(raised, axis=0, keepdims=True)
        grad_probs = dot(value, g, (1, 1))
        delta = jnp.sum(grad_probs * probs, axis=0, keepdims=True)
        grad_scores = (probs * (grad_probs - delta) * scale).astype(BF16)
        gquery[:, cols] = dot(grad_scores, key, (0, 0)).astype(BF16)
        grads[0, :, :, cols] = dot(grad_scores, q, (1, 0)).astype(BF16).reshape(pieces, ROWS, HEAD_DIM)
        grads[1, :, :, cols] = dot(probs.astype(BF16), g, (1, 0)).astype(BF16).reshape(pieces, ROWS, HEAD_DIM)
        return 0

    lax.fori_loop(0, width // HEAD_DIM, attention, 0)

    def finish_grads(i, base, held):
        gfull[i, pl.ds(base, held)] = grads[i, pl.ds(base, held)]

    grad_sum = reduce_gather(grads, ghalves, gfull, g_send, g_recv, finish_grads)
    next(grad_sum)
    span = 8 * wq.shape[1]

    def back(rows, first, last, out):
        def body(t, _):
            wide = wq[pl.ds(t * 8, 8)].reshape(span, width)
            cols = pl.ds(pl.multiple_of(t * span, 128), span)
            left = gquery[pl.ds(pl.multiple_of(rows * toks, toks), toks), :]
            out[:, cols] = dot(left, wide, (1, 1)).astype(out.dtype)
            return 0

        lax.fori_loop(first, last, body, 0)

    tiles = n // 8
    back(other, 0, tiles // 2, gv_send)
    drain(grad_sum, 1)
    back(other, tiles // 2, tiles, gv_send)
    gv_copy = send(gv_send, gv_recv, end_send.at[0], end_recv.at[0], sibling)
    drain(grad_sum, 1)
    for t in range(tiles):
        back(core, t, t + 1, gv_own)
        drain(grad_sum, 1)
    gv_copy.wait_recv()
    grad_video[...] = (gv_own[...] + gv_recv[...].astype(F32)).astype(BF16)
    drain(grad_sum)

    gk, gv = gfull[0].reshape(text_len, width), gfull[1].reshape(text_len, width)
    tail_send[0] = dot(gk, wk[other], (1, 1)) + dot(gv, wv[other], (1, 1))
    stat = jnp.sum(
        gk.astype(F32) * keys[0].reshape(text_len, width).astype(F32)
        + gv.astype(F32) * keys[1].reshape(text_len, width).astype(F32),
        axis=1, keepdims=True,
    )
    tail_send[1] = jnp.broadcast_to(stat, tail_send.shape[1:])
    last = send(tail_send, tail_recv, end_send.at[1], end_recv.at[1], sibling)
    own = dot(gk, wk[core], (1, 1)) + dot(gv, wv[core], (1, 1))
    last.wait_recv()
    grad_normed[...] = own + tail_recv[0]
    row_stat[...] = (tail_send[1] + tail_recv[1])[:, 0:128]
    for copy in pending:
        copy.wait_send()


def body(n, heads_split, text_dim, video, cotangent, text_embed, text_gain, w_query, w_key, w_value, w_out):
    toks, model = video.shape
    text_len, feats = text_embed.shape
    rows = w_query.shape[0]
    width = w_query.shape[1] // 2
    n_bits = int(math.log2(n // 2))
    pieces = text_len // ROWS
    text_wide = text_embed.astype(F32)
    scaled = (text_wide * text_gain).astype(BF16)
    squares = jnp.broadcast_to(jnp.sum(text_wide * text_wide, axis=1, keepdims=True), (text_len, 128))
    lanes = -(-feats // 128) * 128
    if lanes > feats:
        scaled = jnp.pad(scaled, ((0, 0), (0, lanes - feats)))
        w_key, w_value = (jnp.pad(w, ((0, lanes - feats), (0, 0))) for w in (w_key, w_value))
    vmem, dma = pltpu.VMEM, pltpu.SemaphoreType.DMA
    landing = pieces + n_bits
    side = 2 * toks
    flops = 6 * side * model * width + 10 * side * text_len * width
    out = pl.pallas_call(
        functools.partial(kernel, n, text_dim),
        out_shape=[
            jax.ShapeDtypeStruct((toks, model), BF16),
            jax.ShapeDtypeStruct((text_len, lanes), F32),
            jax.ShapeDtypeStruct((text_len, 128), F32),
            jax.ShapeDtypeStruct((text_len, 128), F32),
        ],
        in_specs=[pl.BlockSpec(memory_space=pl.ANY)] * 8,
        out_specs=[pl.BlockSpec(memory_space=pltpu.VMEM)] * 4,
        scratch_shapes=[
            vmem((n, rows, width), BF16),
            vmem((n, rows, width), BF16),
            vmem((2, toks, model), BF16),
            vmem((2, toks, model), BF16),
            vmem((2, lanes, width), BF16),
            vmem((2, lanes, width), BF16),
            vmem((2, text_len, lanes), BF16),
            vmem((2 + n_bits, text_len, 128), F32),
            vmem((1 + n_bits, text_len, 128), F32),
            vmem((2, pieces, ROWS, width), BF16),
            vmem((2, landing, ROWS, width), BF16),
            vmem((2, pieces, ROWS, width), BF16),
            vmem((2, pieces, ROWS, width), BF16),
            vmem((2, landing, ROWS, width), BF16),
            vmem((2, pieces, ROWS, width), BF16),
            vmem((side, width), BF16),
            vmem((side, width), BF16),
            vmem((side, width), BF16),
            vmem((toks, model), BF16),
            vmem((toks, model), BF16),
            vmem((toks, model), F32),
            vmem((2, text_len, lanes), F32),
            vmem((2, text_len, lanes), F32),
            dma((8,)),
            dma((8,)),
            dma((8,)),
            dma((2, 2, n // 2)),
            dma((2, 2, n // 2)),
            dma((n_bits,)),
            dma((n_bits,)),
            dma((2, 2 * n_bits)),
            dma((2, 2 * n_bits)),
            dma((2, 2 * n_bits)),
            dma((2, 2 * n_bits)),
            dma((2,)),
            dma((2,)),
        ],
        compiler_params=pltpu.CompilerParams(
            collective_id=0, has_side_effects=True, vmem_limit_bytes=60 * 1024 * 1024
        ),
        cost_estimate=pl.CostEstimate(
            flops=flops, bytes_accessed=8 * toks * model, transcendentals=side * text_len * width // HEAD_DIM
        ),
    )(scaled, squares, w_key, w_value, w_query, w_out.T, video, cotangent)
    grad_video, grad_normed, row_stat, inverse = out
    grad_normed = grad_normed[:, 0:feats]
    if heads_split > 1:
        grad_normed, row_stat = lax.psum((grad_normed, row_stat), "head")
        grad_video = lax.psum_scatter(grad_video, "head", scatter_dimension=1, tiled=True)
    inv = inverse[:, 0:1]
    grad_text = inv * (grad_normed * text_gain - text_wide * inv * (row_stat[:, 0:1] / text_dim))
    return (grad_video, grad_text)


def solution(mesh):
    n, heads_split = mesh.shape["seq"], mesh.shape["head"]
    in_specs = (
        P("seq", None),
        P("seq", None),
        P(None, "seq"),
        P("seq"),
        P("seq", "head"),
        P("seq", "head"),
        P("seq", "head"),
        P("head", "seq"),
    )
    out_specs = (P("seq", "head"), P(None, "seq"))

    def whole(video, cotangent, text_embed, *rest):
        run = functools.partial(body, n, heads_split, text_embed.shape[1])
        mapped = jax.shard_map(run, mesh=mesh, in_specs=in_specs, out_specs=out_specs, check_vma=False)
        return mapped(video, cotangent, text_embed, *rest)

    return whole
```

time: 656 us -> 275 us (0.42)
  waiting for transfers between devices: 350 us -> 0 us
  Pallas kernels: 0 us -> 265 us
  blocking collectives: 202 us -> 0 us
  matrix products: 72.5 us -> 0 us
  between operations: 13.8 us -> 0.66 us
  local copies, waits for them, and re-layouts: 11.5 us -> 3.42 us
    pallas_call x0 -> x1, Pallas kernels: none -> 265 us  [body(): pl.pallas_call(functools.partial(kernel, n, text_dim), out_shape=[jax.Sha...]
    all_gather x2 -> x0, waiting for transfers between devices: 235 us -> none  [the longest x1 121 us: body(): lax.all_gather(w_out, 'seq', axis=1, tiled=True)]
    psum x3 -> x0, blocking collectives: 202 us -> none  [the longest x1 119 us: body(): grad_keys, grad_values = lax.psum((grad_key_part, grad_value_part), 'seq')]
    psum x1 -> x0, waiting for transfers between devices: 114 us -> none  [body(): lax.psum((key_part, value_part, square_part), 'seq')]
    dot_general x12 -> x0, matrix products: 72.5 us -> none  [the longest x1 13 us: body(): jnp.einsum('htl,thd->lhd', grad_scores, query_heads, preferred_element_ty...]
    reshape x3 -> x0, local copies, waits for them, and re-layouts: 6.92 us -> none  [the longest x1 2.6 us: body(): key_heads = keys.reshape(text_rows, local_heads, HEAD_DIM)]
  transfers between devices with their start and end apart: 3 -> 0, of which waited for: 3 -> 0; matrix products, arithmetic and copies ran while one was open for 3% -> 0% of each run, Pallas kernels for 0% -> 0%
where the time goes in v1:
time: 275 us; the launch traced here: 273 us
  Pallas kernels  265 us (96%)
  other arithmetic  4.3 us (2%)
  local copies, waits for them, and re-layouts  3.42 us (1%)
    pallas_call x1, Pallas kernels, body(): pl.pallas_call(functools.partial(kernel, n, text_dim), out_shape=[jax.Sha...  265 us

profile of v1, /device:TPU:4, one launch (start us, length us, event | category | flops | bytes accessed | tf_op | source)
XLA Modules:
  0.0 273.1 jit_solution(3639917984089147168)
XLA Ops:
  0.6 1.5 fusion.1
  2.1 0.8 broadcast_in_dim.2.squares
  2.9 0.0 copy-start
  2.9 0.0 copy-start.1
  2.9 264.7 %shard_map.95 = (bf16[256,3072]{1,0:T(8,128)(2,1)}, f32[256,128]{1,0:T(8,128)}, f32[256,128]{1,0:T(8,128)}, f32[256,128]{1,0:T(8,128)}) custom-call(bf16[256,128]{1,0:T(8,128)(2,1)} %get-tuple-element.11.scaled, f32[256,128]{1,0:T(8,128)} %broadcast_in_dim.2.squares, bf16[128,3072]{1,0:T(8,128)(2,1)} %w_key.1, bf16[128,3072]{1,0:T(8,128)(2,1)} %w_value.1, ...), custom_call_target="tpu_custom_call" | custom-call | flops 16508780544 | bytes 6291456 | tf_op jit(solution)/shard_map/pallas_call | solution.py:305
  267.6 1.1 multiply_reduce_fusion
  268.7 0.0 copy-done
  268.7 0.0 copy-done.1
  268.7 1.7 fusion.4
  270.4 2.7 copy.11
Async XLA Ops:
  2.9 265.8 %copy-start = (bf16[256,128]{1,0:T(8,128)(2,1)S(1)}, bf16[256,128]{1,0:T(8,128)(2,1)}, u32[]{:S(2)}) copy-start(bf16[256,128]{1,0:T(8,128)(2,1)} %param.10) | copy-start | bytes 196612
  2.9 265.8 %copy-start.1 = (f32[128]{0:T(128)S(1)}, f32[128]{0:T(128)}, u32[]{:S(2)}) copy-start(f32[128]{0:T(128)} %param.11) | copy-start | bytes 1540

commit v2 on v1

v2 whole, which is shorter than its diff:
```python
import functools
import math

import jax
import jax.numpy as jnp
from jax import lax
from jax.experimental import pallas as pl
from jax.experimental.pallas import tpu as pltpu
from jax.sharding import PartitionSpec as P

HEAD_DIM = 128
ROWS = 16
MESH = pl.DeviceIdType.MESH
epsilon = 1e-06
F32 = jnp.float32
BF16 = jnp.bfloat16


def dot(a, b, dims):
    return lax.dot_general(a, b, ((dims[0:1], dims[1:2]), ((), ())), preferred_element_type=F32)


def kernel(
    n, size, text_dim, scaled, squares, w_key, w_value, w_query, w_out, video, cotangent,
    grad_video, grad_normed, row_stat, inverse,
    wq, wo, vid, cot, wk, wv, st, sq, sq_in,
    sums, halves, keys, grads, gstage, ghalves, gfull, query, gout, gquery,
    gv_send, gv_recv, gv_far, gv_own, far_send, far_recv, tail_send, tail_recv, stat_send, stat_recv,
    pair_send, pair_recv, local_sem, act_send, act_recv, w_send, w_recv, sq_send, sq_recv,
    k_send, k_recv, g_send, g_recv, gv_sem, gv_rsem, far_sem, far_rsem, end_send, end_recv,
):
    me = lax.axis_index("seq")
    group, member = me // size, me % size
    core = me % 2
    sibling = me + 1 - 2 * core
    groups = n // size
    n_bits = int(math.log2(groups))
    bit = [(group // (1 << b)) % 2 for b in range(n_bits)]
    partner = [me + (1 - 2 * bit[b]) * (size << b) for b in range(n_bits)]
    side = member // 2
    mates = []
    for d in range(size):
        mate = member
        if d & 1:
            mate = mate + 1 - 2 * core
        if d & 2:
            mate = mate + 2 - 4 * side
        mates.append(mate)
    mate_device = [group * size + mate for mate in mates]
    near_bits = 2 if size == 2 else 1
    low = list(range(min(near_bits, n_bits)))
    high = list(range(len(low), n_bits))
    gather_order = [high + low, high + low[::-1]]
    reduce_order = [low + high, low[::-1] + high if size == 2 else high + low]
    width = wq.shape[2]
    toks = vid.shape[1]
    pending = []

    barrier = pltpu.get_barrier_semaphore()
    peers = mate_device[1:] + partner
    for peer in peers:
        pl.semaphore_signal(barrier, inc=1, device_id={"seq": peer}, device_id_type=MESH)
    pl.semaphore_wait(barrier, len(peers))

    def send(src, dst, send_sem, recv_sem, peer):
        copy = pltpu.make_async_remote_copy(
            src_ref=src, dst_ref=dst, send_sem=send_sem, recv_sem=recv_sem,
            device_id={"seq": peer}, device_id_type=MESH,
        )
        copy.start()
        pending.append(copy)
        return copy

    def part(array):
        return [array.at[:, pl.ds(pl.multiple_of(mate * width, 128), width)] for mate in mates]

    plan = [
        ([scaled] * size, st.at[member]),
        (part(w_key), wk.at[member]),
        (part(w_value), wv.at[member]),
        ([squares] * size, sq.at[member]),
        (part(w_query), wq.at[me]),
        (part(w_out), wo.at[me]),
    ]
    shared = []
    for i, (sources, dst) in enumerate(plan):
        copies = [
            send(sources[d], dst, pair_send.at[i, d], pair_recv.at[i, d], mate_device[d]) for d in range(1, size)
        ]
        local = pltpu.make_async_copy(sources[0], dst, local_sem.at[i])
        local.start()
        shared.append((copies, local))
    moving = []
    for i, (rows, buffer) in enumerate(((video, vid), (cotangent, cot))):
        dst = buffer.at[member]
        copies = [send(rows, dst, act_send.at[i, d], act_recv.at[i, d], mate_device[d]) for d in range(1, min(size, 3))]
        local = pltpu.make_async_copy(rows, dst, local_sem.at[len(plan) + i])
        local.start()
        moving.append((copies, local))

    def have(i):
        for copy in shared[i][0]:
            copy.wait_recv()
        shared[i][1].wait()

    def pass_on(i):
        if size > 2:
            moving[i][0][1].wait_recv()
            rows = (vid, cot)[i].at[mates[2]]
            moving[i][0].append(send(rows, rows, act_send.at[i, 3], act_recv.at[i, 3], mate_device[1]))

    def have_rows(i):
        copies, local = moving[i]
        copies[0].wait_recv()
        if size > 2:
            copies[2].wait_recv()
        local.wait()

    arrivals = {}

    def weights(array, buffer, p):
        for stream in range(size):
            order = gather_order[stream % 2]
            where = group
            for t in range(n_bits):
                if (p >> t) & 1:
                    where = where + (1 - 2 * bit[order[t]]) * (1 << order[t])
            block = buffer.at[size * where + stream]
            if p > 0:
                arrivals[array, stream, p].wait_recv()
            for t in range(p.bit_length(), n_bits):
                q = p + (1 << t)
                arrivals[array, stream, q] = send(
                    block, block, w_send.at[array, stream, q], w_recv.at[array, stream, q], partner[order[t]]
                )

    def reduce_gather(parts, stage, landing, full, send_sem, recv_sem, finish):
        held = parts.shape[1]
        base = [0, 0]
        sizes, bases = [], []
        offset = 0
        for step in range(n_bits):
            half = max(held // 2, 1)
            sent = []
            for i in range(2):
                b = reduce_order[i][step]
                if held > 1:
                    away = base[i] + (1 - bit[b]) * half
                    base[i] = base[i] + bit[b] * half
                else:
                    away = base[i]
                source = parts.at[i, pl.ds(away, half)]
                if stage is not None:
                    stage[i, offset : offset + half] = source[...].astype(stage.dtype)
                    source = stage.at[i, pl.ds(offset, half)]
                sent.append(
                    send(
                        source, landing.at[i, pl.ds(offset, half)],
                        send_sem.at[i, step], recv_sem.at[i, step], partner[b],
                    )
                )
            yield
            for i in range(2):
                sent[i].wait_recv()
                if held == 1:
                    sent[i].wait_send()
                    pending[:] = [copy for copy in pending if copy is not sent[i]]
                spot = pl.ds(base[i], half)
                parts[i, spot] = parts[i, spot] + landing[i, offset : offset + half].astype(F32)
            sizes.append((step, half) if held > 1 else None)
            bases.append(list(base))
            offset += half
            held = half
        for i in range(2):
            finish(i, base[i], held)
        for entry in range(n_bits - 1, -1, -1):
            if sizes[entry] is None:
                continue
            step, half = sizes[entry]
            sent = []
            for i in range(2):
                spot = full.at[i, pl.ds(bases[entry][i], half)]
                sent.append(
                    send(
                        spot, spot, send_sem.at[i, n_bits + step], recv_sem.at[i, n_bits + step],
                        partner[reduce_order[i][step]],
                    )
                )
            yield
            for i in range(2):
                sent[i].wait_recv()

    def square_sum():
        have(3)
        sq_in[0] = functools.reduce(jnp.add, [sq[m] for m in range(size)])
        for b in range(n_bits):
            copy = send(sq_in.at[b], sq.at[size + b], sq_send.at[b], sq_recv.at[b], partner[b])
            yield
            copy.wait_recv()
            sq_in[b + 1] = sq_in[b] + sq[size + b]
        inverse[...] = lax.rsqrt(sq_in[n_bits] / text_dim + epsilon)

    def drain(generator, steps=None):
        count = 0
        for _ in generator:
            count += 1
            if steps is not None and count >= steps:
                return

    pieces = sums.shape[1]
    for i in range(3):
        have(i)
    for i, w in ((0, wk), (1, wv)):
        total = functools.reduce(jnp.add, [dot(st[m], w[m], (1, 0)) for m in range(size)])
        sums[i] = total.reshape(pieces, ROWS, width)

    def finish_keys(i, base, held):
        inv = inverse[pl.ds(pl.multiple_of(base * ROWS, ROWS), held * ROWS), :][:, 0:1]
        total = sums[i, pl.ds(base, held)].reshape(held * ROWS, width)
        keys[i, pl.ds(base, held)] = (inv * total).astype(BF16).reshape(held, ROWS, width)

    text_sum = reduce_gather(sums, None, halves, keys, k_send, k_recv, finish_keys)
    norm_sum = square_sum()
    next(text_sum)
    next(norm_sum)
    have(4)
    weights(0, wq, 0)
    have(5)
    weights(1, wo, 0)
    blocks = 1 << n_bits
    near = blocks // 2
    small = [(0, wq, p) for p in range(1, near)] + [(1, wo, p) for p in range(1, near)]
    for i, event in enumerate(small):
        weights(*event)
        drain(norm_sum, 1)
        drain(text_sum, 1)
        if i == near - 2:
            pass_on(0)
    drain(norm_sum)
    drain(text_sum)
    pass_on(1)
    for p in range(near, blocks):
        weights(0, wq, p)
    have_rows(0)
    tile = 256 if width % 256 == 0 else 128

    def project(rows, w, out):
        def body(t, _):
            cols = pl.ds(pl.multiple_of(t * tile, tile), tile)
            wide = w[:, :, cols].reshape(-1, tile)
            out[:, cols] = dot(rows[...].reshape(size * toks, -1), wide, (1, 0)).astype(BF16)
            return 0

        lax.fori_loop(0, width // tile, body, 0)

    project(vid, wq, query)
    for p in range(near, blocks):
        weights(1, wo, p)
    have_rows(1)
    project(cot, wo, gout)

    scale = HEAD_DIM ** (-0.5)
    text_len = pieces * ROWS

    def attention(h, _):
        cols = pl.ds(pl.multiple_of(h * HEAD_DIM, HEAD_DIM), HEAD_DIM)
        key = keys[0, :, :, cols].reshape(text_len, HEAD_DIM)
        value = keys[1, :, :, cols].reshape(text_len, HEAD_DIM)
        q, g = query[:, cols], gout[:, cols]
        raised = jnp.exp(dot(key, q, (1, 1)) * scale)
        probs = raised / jnp.sum(raised, axis=0, keepdims=True)
        grad_probs = dot(value, g, (1, 1))
        delta = jnp.sum(grad_probs * probs, axis=0, keepdims=True)
        grad_scores = (probs * (grad_probs - delta) * scale).astype(BF16)
        gquery[:, cols] = dot(grad_scores, key, (0, 0)).astype(BF16)
        grads[0, :, :, cols] = dot(grad_scores, q, (1, 0)).reshape(pieces, ROWS, HEAD_DIM)
        grads[1, :, :, cols] = dot(probs.astype(BF16), g, (1, 0)).reshape(pieces, ROWS, HEAD_DIM)
        return 0

    lax.fori_loop(0, width // HEAD_DIM, attention, 0)

    def finish_grads(i, base, held):
        gfull[i, pl.ds(base, held)] = grads[i, pl.ds(base, held)].astype(BF16)

    grad_sum = reduce_gather(grads, gstage, ghalves, gfull, g_send, g_recv, finish_grads)
    next(grad_sum)
    span = 8 * wq.shape[1]
    tiles = n // 8
    chips = size // 2

    def back(who, t):
        wide = wq[8 * t : 8 * t + 8].reshape(span, width)
        left = gquery[pl.ds(pl.multiple_of(who * toks, toks), toks), :]
        return dot(left, wide, (1, 1))

    across, beyond = [], []

    def hand_over(t):
        cols = slice(t * span, (t + 1) * span)
        across[t].wait_recv()
        if chips > 1:
            far_send[t] = (gv_far[:, cols] + gv_recv[t, 1 - side].astype(F32)).astype(BF16)
            beyond.append(send(far_send.at[t], far_recv.at[t], far_sem.at[t], far_rsem.at[t], mate_device[2]))

    for t in range(tiles):
        cols = slice(t * span, (t + 1) * span)
        for x in range(chips):
            gv_send[t, x] = back(2 * x + 1 - core, t).astype(BF16)
        across.append(send(gv_send.at[t], gv_recv.at[t], gv_sem.at[t], gv_rsem.at[t], sibling))
        if chips > 1:
            gv_far[:, cols] = back(mates[2], t)
        drain(grad_sum, 1)
        if t > 0:
            hand_over(t - 1)
    hand_over(tiles - 1)
    for t in range(tiles):
        gv_own[:, t * span : (t + 1) * span] = back(member, t)
        drain(grad_sum, 1)
    drain(grad_sum)

    gk, gv = gfull[0].reshape(text_len, width), gfull[1].reshape(text_len, width)
    products = gk.astype(F32) * keys[0].reshape(text_len, width).astype(F32) + gv.astype(F32) * keys[1].reshape(
        text_len, width
    ).astype(F32)
    stat_send[...] = lax.dot_general(
        jnp.ones((8, width), F32), products, (((1,), (1,)), ((), ())),
        precision=lax.Precision.HIGHEST, preferred_element_type=F32,
    )
    ends = []
    for d in range(size - 1, 0, -1):
        tail_send[d - 1] = (dot(gk, wk[mates[d]], (1, 1)) + dot(gv, wv[mates[d]], (1, 1))).astype(BF16)
        ends.append(send(tail_send.at[d - 1], tail_recv.at[d - 1], end_send.at[0, d], end_recv.at[0, d], mate_device[d]))
        ends.append(send(stat_send, stat_recv.at[d - 1], end_send.at[1, d], end_recv.at[1, d], mate_device[d]))
    total = dot(gk, wk[member], (1, 1)) + dot(gv, wv[member], (1, 1))
    for t in range(tiles):
        cols = slice(t * span, (t + 1) * span)
        tile_sum = gv_own[:, cols] + gv_recv[t, side].astype(F32)
        if chips > 1:
            beyond[t].wait_recv()
            tile_sum = tile_sum + far_recv[t].astype(F32)
        grad_video[:, cols] = tile_sum.astype(BF16)
    for copy in ends:
        copy.wait_recv()
    stat = stat_send[...]
    for d in range(1, size):
        total = total + tail_recv[d - 1].astype(F32)
        stat = stat + stat_recv[d - 1]
    grad_normed[...] = total
    row_stat[...] = stat
    for copy in pending:
        copy.wait_send()


def body(n, heads_split, text_dim, video, cotangent, text_embed, text_gain, w_query, w_key, w_value, w_out):
    toks, model = video.shape
    text_len, feats = text_embed.shape
    rows = w_query.shape[0]
    heads = w_query.shape[1] // HEAD_DIM
    size = 4 if heads % 4 == 0 and n % 4 == 0 else 2
    width = w_query.shape[1] // size
    n_bits = int(math.log2(n // size))
    chips, tiles = size // 2, n // 8
    pieces = text_len // ROWS
    text_wide = text_embed.astype(F32)
    scaled = (text_wide * text_gain).astype(BF16)
    squares = jnp.broadcast_to(jnp.sum(text_wide * text_wide, axis=1, keepdims=True), (text_len, 128))
    lanes = -(-feats // 128) * 128
    if lanes > feats:
        scaled = jnp.pad(scaled, ((0, 0), (0, lanes - feats)))
        w_key, w_value = (jnp.pad(w, ((0, lanes - feats), (0, 0))) for w in (w_key, w_value))
    vmem, dma = pltpu.VMEM, pltpu.SemaphoreType.DMA
    landing = pieces + n_bits
    side = size * toks
    flops = 6 * side * model * width + 10 * side * text_len * width
    out = pl.pallas_call(
        functools.partial(kernel, n, size, text_dim),
        out_shape=[
            jax.ShapeDtypeStruct((toks, model), BF16),
            jax.ShapeDtypeStruct((text_len, lanes), F32),
            jax.ShapeDtypeStruct((8, text_len), F32),
            jax.ShapeDtypeStruct((text_len, 128), F32),
        ],
        in_specs=[pl.BlockSpec(memory_space=pl.ANY)] * 8,
        out_specs=[pl.BlockSpec(memory_space=pltpu.VMEM)] * 4,
        scratch_shapes=[
            vmem((n, rows, width), BF16),
            vmem((n, rows, width), BF16),
            vmem((size, toks, model), BF16),
            vmem((size, toks, model), BF16),
            vmem((size, lanes, width), BF16),
            vmem((size, lanes, width), BF16),
            vmem((size, text_len, lanes), BF16),
            vmem((size + n_bits, text_len, 128), F32),
            vmem((1 + n_bits, text_len, 128), F32),
            vmem((2, pieces, ROWS, width), F32),
            vmem((2, landing, ROWS, width), F32),
            vmem((2, pieces, ROWS, width), BF16),
            vmem((2, pieces, ROWS, width), F32),
            vmem((2, landing, ROWS, width), BF16),
            vmem((2, landing, ROWS, width), BF16),
            vmem((2, pieces, ROWS, width), BF16),
            vmem((side, width), BF16),
            vmem((side, width), BF16),
            vmem((side, width), BF16),
            vmem((tiles, chips, toks, model // tiles), BF16),
            vmem((tiles, chips, toks, model // tiles), BF16),
            vmem((toks, model), F32),
            vmem((toks, model), F32),
            vmem((tiles, toks, model // tiles), BF16),
            vmem((tiles, toks, model // tiles), BF16),
            vmem((size - 1, text_len, lanes), BF16),
            vmem((size - 1, text_len, lanes), BF16),
            vmem((8, text_len), F32),
            vmem((size - 1, 8, text_len), F32),
            dma((6, size)),
            dma((6, size)),
            dma((8,)),
            dma((2, 4)),
            dma((2, 4)),
            dma((2, size, n // size)),
            dma((2, size, n // size)),
            dma((n_bits,)),
            dma((n_bits,)),
            dma((2, 2 * n_bits)),
            dma((2, 2 * n_bits)),
            dma((2, 2 * n_bits)),
            dma((2, 2 * n_bits)),
            dma((tiles,)),
            dma((tiles,)),
            dma((tiles,)),
            dma((tiles,)),
            dma((2, size)),
            dma((2, size)),
        ],
        compiler_params=pltpu.CompilerParams(
            collective_id=0, has_side_effects=True, vmem_limit_bytes=60 * 1024 * 1024
        ),
        cost_estimate=pl.CostEstimate(
            flops=flops, bytes_accessed=8 * toks * model, transcendentals=side * text_len * width // HEAD_DIM
        ),
    )(scaled, squares, w_key, w_value, w_query, w_out.T, video, cotangent)
    grad_video, grad_normed, row_stat, inverse = out
    grad_normed = grad_normed[:, 0:feats]
    if heads_split > 1:
        grad_normed, row_stat = lax.psum((grad_normed, row_stat), "head")
        grad_video = lax.psum_scatter(grad_video, "head", scatter_dimension=1, tiled=True)
    inv = inverse[:, 0:1]
    grad_text = inv * (grad_normed * text_gain - text_wide * inv * (row_stat[0][:, None] / text_dim))
    return (grad_video, grad_text)


def solution(mesh):
    n, heads_split = mesh.shape["seq"], mesh.shape["head"]
    in_specs = (
        P("seq", None),
        P("seq", None),
        P(None, "seq"),
        P("seq"),
        P("seq", "head"),
        P("seq", "head"),
        P("seq", "head"),
        P("head", "seq"),
    )
    out_specs = (P("seq", "head"), P(None, "seq"))

    def whole(video, cotangent, text_embed, *rest):
        run = functools.partial(body, n, heads_split, text_embed.shape[1])
        mapped = jax.shard_map(run, mesh=mesh, in_specs=in_specs, out_specs=out_specs, check_vma=False)
        return mapped(video, cotangent, text_embed, *rest)

    return whole
```

time: 275 us -> 261 us (0.949)
  Pallas kernels: 265 us -> 250 us
    pallas_call x1, Pallas kernels: 265 us -> 250 us  [body(): pl.pallas_call(functools.partial(kernel, n, size, text_dim), out_shape=[j...]
where the time goes in v2:
time: 261 us; the launch traced here: 259 us
  Pallas kernels  250 us (96%)
  local copies, waits for them, and re-layouts  4.42 us (2%)
  other arithmetic  3.89 us (1%)
    pallas_call x1, Pallas kernels, body(): pl.pallas_call(functools.partial(kernel, n, size, text_dim), out_shape=[j...  250 us

profile of v2, /device:TPU:4, one launch (start us, length us, event | category | flops | bytes accessed | tf_op | source)
XLA Modules:
  0.0 258.7 jit_solution(721047588896019687)
XLA Ops:
  0.6 1.5 fusion.1
  2.1 0.8 broadcast_in_dim.2.squares
  2.9 0.0 copy-start
  2.9 0.0 copy-start.1
  2.9 249.8 %shard_map.95 = (bf16[256,3072]{1,0:T(8,128)(2,1)}, f32[256,128]{1,0:T(8,128)}, f32[8,256]{1,0:T(8,128)}, f32[256,128]{1,0:T(8,128)}) custom-call(bf16[256,128]{1,0:T(8,128)(2,1)} %get-tuple-element.11.scaled, f32[256,128]{1,0:T(8,128)} %broadcast_in_dim.2.squares, bf16[128,3072]{1,0:T(8,128)(2,1)} %w_key.1, bf16[128,3072]{1,0:T(8,128)(2,1)} %w_value.1, ...), custom_call_target="tpu_custom_call" | custom-call | flops 16508780544 | bytes 6291456 | tf_op jit(solution)/shard_map/pallas_call | solution.py:375
  252.6 0.7 slice_multiply_fusion
  253.3 1.0 slice_reduce_fusion
  254.4 0.0 copy-done
  254.4 0.0 copy-done.1
  254.4 1.7 fusion.4
  256.1 2.7 %copy.11 = bf16[256,3072]{1,0:T(8,128)(2,1)} copy(bf16[256,3072]{1,0:T(8,128)(2,1)} %get-tuple-element.14) | data formatting | bytes 3145728
Async XLA Ops:
  2.9 251.5 %copy-start = (bf16[256,128]{1,0:T(8,128)(2,1)S(1)}, bf16[256,128]{1,0:T(8,128)(2,1)}, u32[]{:S(2)}) copy-start(bf16[256,128]{1,0:T(8,128)(2,1)} %param.10) | copy-start | bytes 196612
  2.9 251.5 %copy-start.1 = (f32[128]{0:T(128)S(1)}, f32[128]{0:T(128)}, u32[]{:S(2)}) copy-start(f32[128]{0:T(128)} %param.11) | copy-start | bytes 1540

commit v3 on v2

--- a/solution.py
+++ b/solution.py
@@ -244,77 +244,94 @@
     have_rows(0)
     tile = 256 if width % 256 == 0 else 128
 
-    def project(rows, w, out):
+    chips = size // 2
+    span_rows = 2 * toks
+
+    def of_chip(x):
+        return pl.ds(pl.multiple_of(x * span_rows, span_rows), span_rows)
+
+    def project(rows, w, out, first, count):
         def body(t, _):
             cols = pl.ds(pl.multiple_of(t * tile, tile), tile)
             wide = w[:, :, cols].reshape(-1, tile)
-            out[:, cols] = dot(rows[...].reshape(size * toks, -1), wide, (1, 0)).astype(BF16)
+            left = rows[pl.ds(first, count)].reshape(count * toks, -1)
+            out[pl.ds(pl.multiple_of(first * toks, toks), count * toks), cols] = dot(left, wide, (1, 0)).astype(BF16)
             return 0
 
         lax.fori_loop(0, width // tile, body, 0)
 
-    project(vid, wq, query)
+    project(vid, wq, query, 0, size)
     for p in range(near, blocks):
         weights(1, wo, p)
     have_rows(1)
-    project(cot, wo, gout)
 
     scale = HEAD_DIM ** (-0.5)
     text_len = pieces * ROWS
 
-    def attention(h, _):
-        cols = pl.ds(pl.multiple_of(h * HEAD_DIM, HEAD_DIM), HEAD_DIM)
-        key = keys[0, :, :, cols].reshape(text_len, HEAD_DIM)
-        value = keys[1, :, :, cols].reshape(text_len, HEAD_DIM)
-        q, g = query[:, cols], gout[:, cols]
-        raised = jnp.exp(dot(key, q, (1, 1)) * scale)
-        probs = raised / jnp.sum(raised, axis=0, keepdims=True)
-        grad_probs = dot(value, g, (1, 1))
-        delta = jnp.sum(grad_probs * probs, axis=0, keepdims=True)
-        grad_scores = (probs * (grad_probs - delta) * scale).astype(BF16)
-        gquery[:, cols] = dot(grad_scores, key, (0, 0)).astype(BF16)
-        grads[0, :, :, cols] = dot(grad_scores, q, (1, 0)).reshape(pieces, ROWS, HEAD_DIM)
-        grads[1, :, :, cols] = dot(probs.astype(BF16), g, (1, 0)).reshape(pieces, ROWS, HEAD_DIM)
-        return 0
-
-    lax.fori_loop(0, width // HEAD_DIM, attention, 0)
+    def attend(x, more):
+        rows = of_chip(x)
+
+        def attention(h, _):
+            cols = pl.ds(pl.multiple_of(h * HEAD_DIM, HEAD_DIM), HEAD_DIM)
+            key = keys[0, :, :, cols].reshape(text_len, HEAD_DIM)
+            value = keys[1, :, :, cols].reshape(text_len, HEAD_DIM)
+            q, g = query[rows, cols], gout[rows, cols]
+            raised = jnp.exp(dot(key, q, (1, 1)) * scale)
+            probs = raised * (1.0 / jnp.sum(raised, axis=0, keepdims=True))
+            grad_probs = dot(value, g, (1, 1))
+            delta = jnp.sum(grad_probs * probs, axis=0, keepdims=True)
+            grad_scores = (probs * (grad_probs - delta) * scale).astype(BF16)
+            gquery[rows, cols] = dot(grad_scores, key, (0, 0)).astype(BF16)
+            gk = dot(grad_scores, q, (1, 0)).reshape(pieces, ROWS, HEAD_DIM)
+            gv = dot(probs.astype(BF16), g, (1, 0)).reshape(pieces, ROWS, HEAD_DIM)
+            grads[0, :, :, cols] = grads[0, :, :, cols] + gk if more else gk
+            grads[1, :, :, cols] = grads[1, :, :, cols] + gv if more else gv
+            return 0
+
+        lax.fori_loop(0, width // HEAD_DIM, attention, 0)
 
     def finish_grads(i, base, held):
         gfull[i, pl.ds(base, held)] = grads[i, pl.ds(base, held)].astype(BF16)
 
-    grad_sum = reduce_gather(grads, gstage, ghalves, gfull, g_send, g_recv, finish_grads)
-    next(grad_sum)
     span = 8 * wq.shape[1]
     tiles = n // 8
-    chips = size // 2
 
     def back(who, t):
         wide = wq[8 * t : 8 * t + 8].reshape(span, width)
         left = gquery[pl.ds(pl.multiple_of(who * toks, toks), toks), :]
         return dot(left, wide, (1, 1))
 
+    def columns(t):
+        return slice(t * span, (t + 1) * span)
+
     across, beyond = [], []
-
-    def hand_over(t):
-        cols = slice(t * span, (t + 1) * span)
-        across[t].wait_recv()
-        if chips > 1:
-            far_send[t] = (gv_far[:, cols] + gv_recv[t, 1 - side].astype(F32)).astype(BF16)
+    if chips > 1:
+        project(cot, wo, gout, 2 - 2 * side, 2)
+        attend(1 - side, False)
+
+        def hand_over(t):
+            across[t].wait_recv()
+            far_send[t] = (gv_far[:, columns(t)] + gv_recv[t, 1].astype(F32)).astype(BF16)
             beyond.append(send(far_send.at[t], far_recv.at[t], far_sem.at[t], far_rsem.at[t], mate_device[2]))
 
+        for t in range(tiles):
+            gv_send[t, 1] = back(mates[3], t).astype(BF16)
+            across.append(send(gv_send.at[t, 1], gv_recv.at[t, 1], gv_sem.at[t, 1], gv_rsem.at[t, 1], sibling))
+            gv_far[:, columns(t)] = back(mates[2], t)
+            if t > 0:
+                hand_over(t - 1)
+        hand_over(tiles - 1)
+    project(cot, wo, gout, 2 * side, 2)
+    attend(side, chips > 1)
+    grad_sum = reduce_gather(grads, gstage, ghalves, gfull, g_send, g_recv, finish_grads)
+    next(grad_sum)
+    near_copies = []
     for t in range(tiles):
-        cols = slice(t * span, (t + 1) * span)
-        for x in range(chips):
-            gv_send[t, x] = back(2 * x + 1 - core, t).astype(BF16)
-        across.append(send(gv_send.at[t], gv_recv.at[t], gv_sem.at[t], gv_rsem.at[t], sibling))
-        if chips > 1:
-            gv_far[:, cols] = back(mates[2], t)
+        gv_send[t, 0] = back(mates[1], t).astype(BF16)
+        near_copies.append(send(gv_send.at[t, 0], gv_recv.at[t, 0], gv_sem.at[t, 0], gv_rsem.at[t, 0], sibling))
         drain(grad_sum, 1)
-        if t > 0:
-            hand_over(t - 1)
-    hand_over(tiles - 1)
     for t in range(tiles):
-        gv_own[:, t * span : (t + 1) * span] = back(member, t)
+        gv_own[:, columns(t)] = back(member, t)
         drain(grad_sum, 1)
     drain(grad_sum)
 
@@ -333,8 +350,9 @@
         ends.append(send(stat_send, stat_recv.at[d - 1], end_send.at[1, d], end_recv.at[1, d], mate_device[d]))
     total = dot(gk, wk[member], (1, 1)) + dot(gv, wv[member], (1, 1))
     for t in range(tiles):
-        cols = slice(t * span, (t + 1) * span)
-        tile_sum = gv_own[:, cols] + gv_recv[t, side].astype(F32)
+        cols = columns(t)
+        near_copies[t].wait_recv()
+        tile_sum = gv_own[:, cols] + gv_recv[t, 0].astype(F32)
         if chips > 1:
             beyond[t].wait_recv()
             tile_sum = tile_sum + far_recv[t].astype(F32)
@@ -425,8 +443,8 @@
             dma((2, 2 * n_bits)),
             dma((2, 2 * n_bits)),
             dma((2, 2 * n_bits)),
-            dma((tiles,)),
-            dma((tiles,)),
+            dma((tiles, 2)),
+            dma((tiles, 2)),
             dma((tiles,)),
             dma((tiles,)),
             dma((2, size)),

time: 261 us -> 264 us (1.011)
  Pallas kernels: 250 us -> 255 us
    pallas_call x1, Pallas kernels: 250 us -> 255 us  [body(): pl.pallas_call(functools.partial(kernel, n, size, text_dim), out_shape=[j...]
where the time goes in v3:
time: 264 us
  Pallas kernels  255 us (97%)
  local copies, waits for them, and re-layouts  4.42 us (2%)
  other arithmetic  3.89 us (1%)
    pallas_call x1, Pallas kernels, body(): pl.pallas_call(functools.partial(kernel, n, size, text_dim), out_shape=[j...  255 us

profile of v3, /device:TPU:4, one launch (start us, length us, event | category | flops | bytes accessed | tf_op | source)
XLA Modules:
  0.0 263.9 jit_solution(6447914430474151247)
XLA Ops:
  0.6 1.5 fusion.1
  2.1 0.8 broadcast_in_dim.2.squares
  2.9 0.0 copy-start
  2.9 0.0 copy-start.1
  2.9 255.0 %shard_map.95 = (bf16[256,3072]{1,0:T(8,128)(2,1)}, f32[256,128]{1,0:T(8,128)}, f32[8,256]{1,0:T(8,128)}, f32[256,128]{1,0:T(8,128)}) custom-call(bf16[256,128]{1,0:T(8,128)(2,1)} %get-tuple-element.11.scaled, f32[256,128]{1,0:T(8,128)} %broadcast_in_dim.2.squares, bf16[128,3072]{1,0:T(8,128)(2,1)} %w_key.1, bf16[128,3072]{1,0:T(8,128)(2,1)} %w_value.1, ...), custom_call_target="tpu_custom_call" | custom-call | flops 16508780544 | bytes 6291456 | tf_op jit(solution)/shard_map/pallas_call | solution.py:393
  257.9 0.7 slice_multiply_fusion
  258.6 1.0 slice_reduce_fusion
  259.6 0.0 copy-done
  259.6 0.0 copy-done.1
  259.6 1.7 fusion.4
  261.3 2.7 %copy.11 = bf16[256,3072]{1,0:T(8,128)(2,1)} copy(bf16[256,3072]{1,0:T(8,128)(2,1)} %get-tuple-element.14) | data formatting | bytes 3145728
Async XLA Ops:
  2.9 256.7 %copy-start = (bf16[256,128]{1,0:T(8,128)(2,1)S(1)}, bf16[256,128]{1,0:T(8,128)(2,1)}, u32[]{:S(2)}) copy-start(bf16[256,128]{1,0:T(8,128)(2,1)} %param.10) | copy-start | bytes 196612
  2.9 256.7 %copy-start.1 = (f32[128]{0:T(128)S(1)}, f32[128]{0:T(128)}, u32[]{:S(2)}) copy-start(f32[128]{0:T(128)} %param.11) | copy-start | bytes 1540

commit v4 on v2

--- a/solution.py
+++ b/solution.py
@@ -24,8 +24,8 @@
     n, size, text_dim, scaled, squares, w_key, w_value, w_query, w_out, video, cotangent,
     grad_video, grad_normed, row_stat, inverse,
     wq, wo, vid, cot, wk, wv, st, sq, sq_in,
-    sums, halves, keys, grads, gstage, ghalves, gfull, query, gout, gquery,
-    gv_send, gv_recv, gv_far, gv_own, far_send, far_recv, tail_send, tail_recv, stat_send, stat_recv,
+    sums, halves, keys, grads, gstage, ghalves, gfull, query, gout, gquery, wqt,
+    gv_send, gv_recv, gv_mine, far_send, far_recv, tail_send, tail_recv, stat_send, stat_recv,
     pair_send, pair_recv, local_sem, act_send, act_recv, w_send, w_recv, sq_send, sq_recv,
     k_send, k_recv, g_send, g_recv, gv_sem, gv_rsem, far_sem, far_rsem, end_send, end_recv,
 ):
@@ -90,13 +90,24 @@
         local = pltpu.make_async_copy(sources[0], dst, local_sem.at[i])
         local.start()
         shared.append((copies, local))
-    moving = []
+    chips = size // 2
+    cuts = 4
+    piece = toks // cuts
+    slots = [(mate % 2) * chips + mate // 2 for mate in mates]
+    moving = [[], []]
+    own_rows = []
     for i, (rows, buffer) in enumerate(((video, vid), (cotangent, cot))):
-        dst = buffer.at[member]
-        copies = [send(rows, dst, act_send.at[i, d], act_recv.at[i, d], mate_device[d]) for d in range(1, min(size, 3))]
-        local = pltpu.make_async_copy(rows, dst, local_sem.at[len(plan) + i])
+        local = pltpu.make_async_copy(rows, buffer.at[slots[0]], local_sem.at[len(plan) + i])
         local.start()
-        moving.append((copies, local))
+        own_rows.append(local)
+
+    def move(i, c):
+        rows, buffer = ((video, vid), (cotangent, cot))[i]
+        cut = pl.ds(c * piece, piece)
+        dst = buffer.at[slots[0], cut]
+        moving[i].append(
+            [send(rows.at[cut], dst, act_send.at[i, c, d], act_recv.at[i, c, d], mate_device[d]) for d in range(min(size, 3) - 1, 0, -1)]
+        )
 
     def have(i):
         for copy in shared[i][0]:
@@ -105,16 +116,17 @@
 
     def pass_on(i):
         if size > 2:
-            moving[i][0][1].wait_recv()
-            rows = (vid, cot)[i].at[mates[2]]
-            moving[i][0].append(send(rows, rows, act_send.at[i, 3], act_recv.at[i, 3], mate_device[1]))
+            for c in range(cuts):
+                copies = moving[i][c]
+                copies[0].wait_recv()
+                rows = (vid, cot)[i].at[slots[2], pl.ds(c * piece, piece)]
+                copies.append(send(rows, rows, act_send.at[i, c, 3], act_recv.at[i, c, 3], mate_device[1]))
 
     def have_rows(i):
-        copies, local = moving[i]
-        copies[0].wait_recv()
-        if size > 2:
-            copies[2].wait_recv()
-        local.wait()
+        for copies in moving[i]:
+            for copy in copies[1:] if size > 2 else copies:
+                copy.wait_recv()
+        own_rows[i].wait()
 
     arrivals = {}
 
@@ -208,37 +220,45 @@
                 return
 
     pieces = sums.shape[1]
+    def finish_keys(i, base, held):
+        inv = inverse[pl.ds(pl.multiple_of(base * ROWS, ROWS), held * ROWS), :][:, 0:1]
+        total = sums[i, pl.ds(base, held)].reshape(held * ROWS, width)
+        keys[i, pl.ds(base, held)] = (inv * total).astype(BF16).reshape(held, ROWS, width)
+
+    text_sum = reduce_gather(sums, None, halves, keys, k_send, k_recv, finish_keys)
+    norm_sum = square_sum()
+    have(4)
+    weights(0, wq, 0)
     for i in range(3):
         have(i)
     for i, w in ((0, wk), (1, wv)):
         total = functools.reduce(jnp.add, [dot(st[m], w[m], (1, 0)) for m in range(size)])
         sums[i] = total.reshape(pieces, ROWS, width)
 
-    def finish_keys(i, base, held):
-        inv = inverse[pl.ds(pl.multiple_of(base * ROWS, ROWS), held * ROWS), :][:, 0:1]
-        total = sums[i, pl.ds(base, held)].reshape(held * ROWS, width)
-        keys[i, pl.ds(base, held)] = (inv * total).astype(BF16).reshape(held, ROWS, width)
-
-    text_sum = reduce_gather(sums, None, halves, keys, k_send, k_recv, finish_keys)
-    norm_sum = square_sum()
     next(text_sum)
     next(norm_sum)
-    have(4)
-    weights(0, wq, 0)
     have(5)
     weights(1, wo, 0)
+    for c in range(cuts):
+        move(0, c)
     blocks = 1 << n_bits
     near = blocks // 2
-    small = [(0, wq, p) for p in range(1, near)] + [(1, wo, p) for p in range(1, near)]
-    for i, event in enumerate(small):
-        weights(*event)
+    for p in range(1, near):
+        weights(0, wq, p)
         drain(norm_sum, 1)
-        drain(text_sum, 1)
-        if i == near - 2:
+        if p >= 2:
+            drain(text_sum, 1)
+        weights(1, wo, p)
+        if p == 1:
+            for c in range(cuts):
+                move(1, c)
+        else:
+            drain(norm_sum, 1)
+            drain(text_sum, 1)
+        if p == 2:
             pass_on(0)
+    pass_on(1)
     drain(norm_sum)
-    drain(text_sum)
-    pass_on(1)
     for p in range(near, blocks):
         weights(0, wq, p)
     have_rows(0)
@@ -254,6 +274,11 @@
         lax.fori_loop(0, width // tile, body, 0)
 
     project(vid, wq, query)
+    span = 8 * wq.shape[1]
+    tiles = n // 8
+    for t in range(tiles):
+        wqt[:, t * span : (t + 1) * span] = wq[8 * t : 8 * t + 8].reshape(span, width).T
+    drain(text_sum)
     for p in range(near, blocks):
         weights(1, wo, p)
     have_rows(1)
@@ -268,7 +293,7 @@
         value = keys[1, :, :, cols].reshape(text_len, HEAD_DIM)
         q, g = query[:, cols], gout[:, cols]
         raised = jnp.exp(dot(key, q, (1, 1)) * scale)
-        probs = raised / jnp.sum(raised, axis=0, keepdims=True)
+        probs = raised * (1.0 / jnp.sum(raised, axis=0, keepdims=True))
         grad_probs = dot(value, g, (1, 1))
         delta = jnp.sum(grad_probs * probs, axis=0, keepdims=True)
         grad_scores = (probs * (grad_probs - delta) * scale).astype(BF16)
@@ -284,38 +309,28 @@
 
     grad_sum = reduce_gather(grads, gstage, ghalves, gfull, g_send, g_recv, finish_grads)
     next(grad_sum)
-    span = 8 * wq.shape[1]
-    tiles = n // 8
-    chips = size // 2
+    half_rows = chips * toks
 
     def back(who, t):
-        wide = wq[8 * t : 8 * t + 8].reshape(span, width)
-        left = gquery[pl.ds(pl.multiple_of(who * toks, toks), toks), :]
-        return dot(left, wide, (1, 1))
+        left = gquery[pl.ds(pl.multiple_of(who * half_rows, half_rows), half_rows), :]
+        return dot(left, wqt[:, t * span : (t + 1) * span], (1, 0)).reshape(chips, toks, span)
 
     across, beyond = [], []
 
     def hand_over(t):
-        cols = slice(t * span, (t + 1) * span)
         across[t].wait_recv()
         if chips > 1:
-            far_send[t] = (gv_far[:, cols] + gv_recv[t, 1 - side].astype(F32)).astype(BF16)
+            far_send[t] = (gv_mine[t, 1 - side] + gv_recv[t, 1 - side].astype(F32)).astype(BF16)
             beyond.append(send(far_send.at[t], far_recv.at[t], far_sem.at[t], far_rsem.at[t], mate_device[2]))
 
     for t in range(tiles):
-        cols = slice(t * span, (t + 1) * span)
-        for x in range(chips):
-            gv_send[t, x] = back(2 * x + 1 - core, t).astype(BF16)
+        gv_send[t] = back(1 - core, t).astype(BF16)
         across.append(send(gv_send.at[t], gv_recv.at[t], gv_sem.at[t], gv_rsem.at[t], sibling))
-        if chips > 1:
-            gv_far[:, cols] = back(mates[2], t)
+        gv_mine[t] = back(core, t)
         drain(grad_sum, 1)
         if t > 0:
             hand_over(t - 1)
     hand_over(tiles - 1)
-    for t in range(tiles):
-        gv_own[:, t * span : (t + 1) * span] = back(member, t)
-        drain(grad_sum, 1)
     drain(grad_sum)
 
     gk, gv = gfull[0].reshape(text_len, width), gfull[1].reshape(text_len, width)
@@ -334,7 +349,7 @@
     total = dot(gk, wk[member], (1, 1)) + dot(gv, wv[member], (1, 1))
     for t in range(tiles):
         cols = slice(t * span, (t + 1) * span)
-        tile_sum = gv_own[:, cols] + gv_recv[t, side].astype(F32)
+        tile_sum = gv_mine[t, side] + gv_recv[t, side].astype(F32)
         if chips > 1:
             beyond[t].wait_recv()
             tile_sum = tile_sum + far_recv[t].astype(F32)
@@ -402,10 +417,10 @@
             vmem((side, width), BF16),
             vmem((side, width), BF16),
             vmem((side, width), BF16),
+            vmem((width, model), BF16),
             vmem((tiles, chips, toks, model // tiles), BF16),
             vmem((tiles, chips, toks, model // tiles), BF16),
-            vmem((toks, model), F32),
-            vmem((toks, model), F32),
+            vmem((tiles, chips, toks, model // tiles), F32),
             vmem((tiles, toks, model // tiles), BF16),
             vmem((tiles, toks, model // tiles), BF16),
             vmem((size - 1, text_len, lanes), BF16),
@@ -415,8 +430,8 @@
             dma((6, size)),
             dma((6, size)),
             dma((8,)),
-            dma((2, 4)),
-            dma((2, 4)),
+            dma((2, 4, 4)),
+            dma((2, 4, 4)),
             dma((2, size, n // size)),
             dma((2, size, n // size)),
             dma((n_bits,)),
@@ -433,7 +448,7 @@
             dma((2, size)),
         ],
         compiler_params=pltpu.CompilerParams(
-            collective_id=0, has_side_effects=True, vmem_limit_bytes=60 * 1024 * 1024
+            collective_id=0, has_side_effects=True, vmem_limit_bytes=63 * 1024 * 1024
         ),
         cost_estimate=pl.CostEstimate(
             flops=flops, bytes_accessed=8 * toks * model, transcendentals=side * text_len * width // HEAD_DIM

time: 261 us -> 265 us (1.015)
  Pallas kernels: 250 us -> 253 us
    pallas_call x1, Pallas kernels: 250 us -> 253 us  [body(): pl.pallas_call(functools.partial(kernel, n, size, text_dim), out_shape=[j...]
where the time goes in v4:
time: 265 us; the launch traced here: 262 us
  Pallas kernels  253 us (95%)
  local copies, waits for them, and re-layouts  4.42 us (2%)
  other arithmetic  3.89 us (1%)
    pallas_call x1, Pallas kernels, body(): pl.pallas_call(functools.partial(kernel, n, size, text_dim), out_shape=[j...  253 us

profile of v4, /device:TPU:4, one launch (start us, length us, event | category | flops | bytes accessed | tf_op | source)
XLA Modules:
  0.0 261.8 jit_solution(60875207469785550)
XLA Ops:
  0.6 1.5 fusion.1
  2.1 0.8 broadcast_in_dim.2.squares
  2.9 0.0 copy-start
  2.9 0.0 copy-start.1
  2.9 252.9 %shard_map.95 = (bf16[256,3072]{1,0:T(8,128)(2,1)}, f32[256,128]{1,0:T(8,128)}, f32[8,256]{1,0:T(8,128)}, f32[256,128]{1,0:T(8,128)}) custom-call(bf16[256,128]{1,0:T(8,128)(2,1)} %get-tuple-element.11.scaled, f32[256,128]{1,0:T(8,128)} %broadcast_in_dim.2.squares, bf16[128,3072]{1,0:T(8,128)(2,1)} %w_key.1, bf16[128,3072]{1,0:T(8,128)(2,1)} %w_value.1, ...), custom_call_target="tpu_custom_call" | custom-call | flops 16508780544 | bytes 6291456 | tf_op jit(solution)/shard_map/pallas_call | solution.py:390
  255.8 0.7 slice_multiply_fusion
  256.5 1.0 slice_reduce_fusion
  257.5 0.0 copy-done
  257.5 0.0 copy-done.1
  257.5 1.7 fusion.4
  259.2 2.7 %copy.11 = bf16[256,3072]{1,0:T(8,128)(2,1)} copy(bf16[256,3072]{1,0:T(8,128)(2,1)} %get-tuple-element.14) | data formatting | bytes 3145728
Async XLA Ops:
  2.9 254.6 %copy-start = (bf16[256,128]{1,0:T(8,128)(2,1)S(1)}, bf16[256,128]{1,0:T(8,128)(2,1)}, u32[]{:S(2)}) copy-start(bf16[256,128]{1,0:T(8,128)(2,1)} %param.10) | copy-start | bytes 196612
  2.9 254.6 %copy-start.1 = (f32[128]{0:T(128)S(1)}, f32[128]{0:T(128)}, u32[]{:S(2)}) copy-start(f32[128]{0:T(128)} %param.11) | copy-start | bytes 1540

commit v5 on v4

--- a/solution.py
+++ b/solution.py
@@ -26,7 +26,7 @@
     wq, wo, vid, cot, wk, wv, st, sq, sq_in,
     sums, halves, keys, grads, gstage, ghalves, gfull, query, gout, gquery, wqt,
     gv_send, gv_recv, gv_mine, far_send, far_recv, tail_send, tail_recv, stat_send, stat_recv,
-    pair_send, pair_recv, local_sem, act_send, act_recv, w_send, w_recv, sq_send, sq_recv,
+    pair_send, pair_recv, local_sem, act_send, act_recv, w_send, w_recv, n_send, n_recv, sq_send, sq_recv,
     k_send, k_recv, g_send, g_recv, gv_sem, gv_rsem, far_sem, far_rsem, end_send, end_recv,
 ):
     me = lax.axis_index("seq")
@@ -50,17 +50,27 @@
     near_bits = 2 if size == 2 else 1
     low = list(range(min(near_bits, n_bits)))
     high = list(range(len(low), n_bits))
-    gather_order = [high + low, high + low[::-1]]
     reduce_order = [low + high, low[::-1] + high if size == 2 else high + low]
     width = wq.shape[2]
     toks = vid.shape[1]
     pending = []
 
+    line = 1 << len(high)
+    near_count = 1 << len(low)
+    place = group // near_count
+    line_peer = (me + size * near_count, me - size * near_count)
     barrier = pltpu.get_barrier_semaphore()
     peers = mate_device[1:] + partner
     for peer in peers:
         pl.semaphore_signal(barrier, inc=1, device_id={"seq": peer}, device_id_type=MESH)
-    pl.semaphore_wait(barrier, len(peers))
+    for more, peer in ((place < line - 1, line_peer[0]), (place > 0, line_peer[1])):
+
+        @pl.when(more)
+        def _():
+            pl.semaphore_signal(barrier, inc=1, device_id={"seq": peer}, device_id_type=MESH)
+
+    ends_count = (place + line - 1) // line + (2 * line - 2 - place) // line
+    pl.semaphore_wait(barrier, len(peers) + ends_count)
 
     def send(src, dst, send_sem, recv_sem, peer):
         copy = pltpu.make_async_remote_copy(
@@ -128,23 +138,88 @@
                 copy.wait_recv()
         own_rows[i].wait()
 
-    arrivals = {}
-
-    def weights(array, buffer, p):
+    late = []
+
+    def when(condition, run):
+        if condition is None:
+            run()
+        else:
+            pl.when(condition)(run)
+
+    def exists(way, k):
+        if k == 0:
+            return None
+        return place >= k if way == 0 else place < line - k
+
+    def block(buffer, stream, way, k, pattern=0):
+        where = group + (k if way else -k) * near_count
+        order = low if stream % 2 == 0 else low[::-1]
+        for t in range(len(low)):
+            if (pattern >> t) & 1:
+                where = where + (1 - 2 * bit[order[t]]) * (1 << order[t])
+        return buffer.at[size * where + stream]
+
+    def line_copy(array, buffer, stream, way, k, at):
+        spot = block(buffer, stream, way, at)
+        i = ((array * size + stream) * 2 + way) * line + k
+        return pltpu.make_async_remote_copy(
+            src_ref=spot, dst_ref=spot, send_sem=w_send.at[i], recv_sem=w_recv.at[i],
+            device_id={"seq": line_peer[way]}, device_id_type=MESH,
+        )
+
+    def near_copy(array, buffer, stream, way, k, pattern, t):
+        spot = block(buffer, stream, way, k, pattern)
+        order = low if stream % 2 == 0 else low[::-1]
+        i = (((array * size + stream) * 2 + way) * line + k) * near_count + pattern + (1 << t)
+        return pltpu.make_async_remote_copy(
+            src_ref=spot, dst_ref=spot, send_sem=n_send.at[i], recv_sem=n_recv.at[i],
+            device_id={"seq": partner[order[t]]}, device_id_type=MESH,
+        )
+
+    def weights(array, buffer, k):
         for stream in range(size):
-            order = gather_order[stream % 2]
-            where = group
-            for t in range(n_bits):
-                if (p >> t) & 1:
-                    where = where + (1 - 2 * bit[order[t]]) * (1 << order[t])
-            block = buffer.at[size * where + stream]
-            if p > 0:
-                arrivals[array, stream, p].wait_recv()
-            for t in range(p.bit_length(), n_bits):
-                q = p + (1 << t)
-                arrivals[array, stream, q] = send(
-                    block, block, w_send.at[array, stream, q], w_recv.at[array, stream, q], partner[order[t]]
-                )
+            for way in (0, 1) if k else (0,):
+
+                def go(stream=stream, way=way):
+                    if k:
+                        line_copy(array, buffer, stream, way, k, k).wait_recv()
+                    if k + 1 < line:
+                        for e in (way,) if k else (0, 1):
+                            more = place < line - 1 if e == 0 else place > 0
+                            when(more, lambda e=e: line_copy(array, buffer, stream, e, k + 1, k).start())
+                    for t in range(len(low)):
+                        near_copy(array, buffer, stream, way, k, 0, t).start()
+
+                def end(stream=stream, way=way):
+                    if k + 1 < line:
+                        for e in (way,) if k else (0, 1):
+                            more = place < line - 1 if e == 0 else place > 0
+                            when(more, lambda e=e: line_copy(array, buffer, stream, e, k + 1, k).wait_send())
+                    for t in range(len(low)):
+                        near_copy(array, buffer, stream, way, k, 0, t).wait_send()
+
+                when(exists(way, k), go)
+                late.append((exists(way, k), end))
+
+    def arrive(array, buffer, k):
+        for stream in range(size):
+            for way in (0, 1) if k else (0,):
+
+                def go(stream=stream, way=way):
+                    for pattern in range(1, near_count):
+                        t = pattern.bit_length() - 1
+                        near_copy(array, buffer, stream, way, k, pattern - (1 << t), t).wait_recv()
+                        for u in range(t + 1, len(low)):
+                            near_copy(array, buffer, stream, way, k, pattern, u).start()
+
+                def end(stream=stream, way=way):
+                    for pattern in range(1, near_count):
+                        for u in range(pattern.bit_length(), len(low)):
+                            near_copy(array, buffer, stream, way, k, pattern, u).wait_send()
+
+                when(exists(way, k), go)
+                if len(low) > 1:
+                    late.append((exists(way, k), end))
 
     def reduce_gather(parts, stage, landing, full, send_sem, recv_sem, finish):
         held = parts.shape[1]
@@ -241,9 +316,7 @@
     weights(1, wo, 0)
     for c in range(cuts):
         move(0, c)
-    blocks = 1 << n_bits
-    near = blocks // 2
-    for p in range(1, near):
+    for p in range(1, line):
         weights(0, wq, p)
         drain(norm_sum, 1)
         if p >= 2:
@@ -259,8 +332,8 @@
             pass_on(0)
     pass_on(1)
     drain(norm_sum)
-    for p in range(near, blocks):
-        weights(0, wq, p)
+    for k in range(line):
+        arrive(0, wq, k)
     have_rows(0)
     tile = 256 if width % 256 == 0 else 128
 
@@ -279,8 +352,8 @@
     for t in range(tiles):
         wqt[:, t * span : (t + 1) * span] = wq[8 * t : 8 * t + 8].reshape(span, width).T
     drain(text_sum)
-    for p in range(near, blocks):
-        weights(1, wo, p)
+    for k in range(line):
+        arrive(1, wo, k)
     have_rows(1)
     project(cot, wo, gout)
 
@@ -362,6 +435,8 @@
         stat = stat + stat_recv[d - 1]
     grad_normed[...] = total
     row_stat[...] = stat
+    for condition, end in late:
+        when(condition, end)
     for copy in pending:
         copy.wait_send()
 
@@ -375,6 +450,7 @@
     width = w_query.shape[1] // size
     n_bits = int(math.log2(n // size))
     chips, tiles = size // 2, n // 8
+    line = n // size // min(n // size, 4 if size == 2 else 2)
     pieces = text_len // ROWS
     text_wide = text_embed.astype(F32)
     scaled = (text_wide * text_gain).astype(BF16)
@@ -432,8 +508,10 @@
             dma((8,)),
             dma((2, 4, 4)),
             dma((2, 4, 4)),
-            dma((2, size, n // size)),
-            dma((2, size, n // size)),
+            dma((4 * size * line,)),
+            dma((4 * size * line,)),
+            dma((4 * n,)),
+            dma((4 * n,)),
             dma((n_bits,)),
             dma((n_bits,)),
             dma((2, 2 * n_bits)),

time: 265 us -> 247 us (0.932); the launches traced: 262 us -> 247 us
  Pallas kernels: 253 us -> 238 us
    pallas_call x1, Pallas kernels: 253 us -> 238 us  [body(): pl.pallas_call(functools.partial(kernel, n, size, text_dim), out_shape=[j...]
where the time goes in v5:
time: 247 us
  Pallas kernels  238 us (96%)
  local copies, waits for them, and re-layouts  4.42 us (2%)
  other arithmetic  3.89 us (2%)
    pallas_call x1, Pallas kernels, body(): pl.pallas_call(functools.partial(kernel, n, size, text_dim), out_shape=[j...  238 us

profile of v5, /device:TPU:4, one launch (start us, length us, event | category | flops | bytes accessed | tf_op | source)
XLA Modules:
  0.0 246.6 jit_solution(6518927002664373149)
XLA Ops:
  0.6 1.5 fusion.1
  2.1 0.8 broadcast_in_dim.2.squares
  2.9 0.0 copy-start
  2.9 0.0 copy-start.1
  2.9 237.6 %shard_map.95 = (bf16[256,3072]{1,0:T(8,128)(2,1)}, f32[256,128]{1,0:T(8,128)}, f32[8,256]{1,0:T(8,128)}, f32[256,128]{1,0:T(8,128)}) custom-call(bf16[256,128]{1,0:T(8,128)(2,1)} %get-tuple-element.11.scaled, f32[256,128]{1,0:T(8,128)} %broadcast_in_dim.2.squares, bf16[128,3072]{1,0:T(8,128)(2,1)} %w_key.1, bf16[128,3072]{1,0:T(8,128)(2,1)} %w_value.1, ...), custom_call_target="tpu_custom_call" | custom-call | flops 16508780544 | bytes 6291456 | tf_op jit(solution)/shard_map/pallas_call | solution.py:466
  240.5 0.7 slice_multiply_fusion
  241.2 1.0 slice_reduce_fusion
  242.2 0.0 copy-done
  242.2 0.0 copy-done.1
  242.2 1.7 fusion.4
  243.9 2.7 %copy.11 = bf16[256,3072]{1,0:T(8,128)(2,1)} copy(bf16[256,3072]{1,0:T(8,128)(2,1)} %get-tuple-element.14) | data formatting | bytes 3145728
Async XLA Ops:
  2.9 239.4 %copy-start = (bf16[256,128]{1,0:T(8,128)(2,1)S(1)}, bf16[256,128]{1,0:T(8,128)(2,1)}, u32[]{:S(2)}) copy-start(bf16[256,128]{1,0:T(8,128)(2,1)} %param.10) | copy-start | bytes 196612
  2.9 239.4 %copy-start.1 = (f32[128]{0:T(128)S(1)}, f32[128]{0:T(128)}, u32[]{:S(2)}) copy-start(f32[128]{0:T(128)} %param.11) | copy-start | bytes 1540

commit v6 on v5

--- a/solution.py
+++ b/solution.py
@@ -360,50 +360,70 @@
     scale = HEAD_DIM ** (-0.5)
     text_len = pieces * ROWS
 
-    def attention(h, _):
-        cols = pl.ds(pl.multiple_of(h * HEAD_DIM, HEAD_DIM), HEAD_DIM)
-        key = keys[0, :, :, cols].reshape(text_len, HEAD_DIM)
-        value = keys[1, :, :, cols].reshape(text_len, HEAD_DIM)
-        q, g = query[:, cols], gout[:, cols]
-        raised = jnp.exp(dot(key, q, (1, 1)) * scale)
-        probs = raised * (1.0 / jnp.sum(raised, axis=0, keepdims=True))
-        grad_probs = dot(value, g, (1, 1))
-        delta = jnp.sum(grad_probs * probs, axis=0, keepdims=True)
-        grad_scores = (probs * (grad_probs - delta) * scale).astype(BF16)
-        gquery[:, cols] = dot(grad_scores, key, (0, 0)).astype(BF16)
-        grads[0, :, :, cols] = dot(grad_scores, q, (1, 0)).reshape(pieces, ROWS, HEAD_DIM)
-        grads[1, :, :, cols] = dot(probs.astype(BF16), g, (1, 0)).reshape(pieces, ROWS, HEAD_DIM)
-        return 0
-
-    lax.fori_loop(0, width // HEAD_DIM, attention, 0)
+    def slot_rows(slot):
+        return pl.ds(pl.multiple_of(slot * toks, toks), toks)
+
+    def attend(x, more):
+        def attention(h, _):
+            cols = pl.ds(pl.multiple_of(h * HEAD_DIM, HEAD_DIM), HEAD_DIM)
+            key = keys[0, :, :, cols].reshape(text_len, HEAD_DIM)
+            value = keys[1, :, :, cols].reshape(text_len, HEAD_DIM)
+            gk, gv = 0.0, 0.0
+            for c in range(2):
+                rows = slot_rows(c * chips + x)
+                q, g = query[rows, cols], gout[rows, cols]
+                raised = jnp.exp(dot(key, q, (1, 1)) * scale)
+                probs = raised * (1.0 / jnp.sum(raised, axis=0, keepdims=True))
+                grad_probs = dot(value, g, (1, 1))
+                delta = jnp.sum(grad_probs * probs, axis=0, keepdims=True)
+                grad_scores = (probs * (grad_probs - delta) * scale).astype(BF16)
+                gquery[rows, cols] = dot(grad_scores, key, (0, 0)).astype(BF16)
+                gk = gk + dot(grad_scores, q, (1, 0))
+                gv = gv + dot(probs.astype(BF16), g, (1, 0))
+            gk, gv = gk.reshape(pieces, ROWS, HEAD_DIM), gv.reshape(pieces, ROWS, HEAD_DIM)
+            grads[0, :, :, cols] = grads[0, :, :, cols] + gk if more else gk
+            grads[1, :, :, cols] = grads[1, :, :, cols] + gv if more else gv
+            return 0
+
+        lax.fori_loop(0, width // HEAD_DIM, attention, 0)
 
     def finish_grads(i, base, held):
         gfull[i, pl.ds(base, held)] = grads[i, pl.ds(base, held)].astype(BF16)
 
+
+    def back(slot, t):
+        return dot(gquery[slot_rows(slot), :], wqt[:, t * span : (t + 1) * span], (1, 0))
+
+    def across_cores(x, place, t):
+        gv_send[t, place] = back((1 - core) * chips + x, t).astype(BF16)
+        return send(
+            gv_send.at[t, place], gv_recv.at[t, place], gv_sem.at[t, place], gv_rsem.at[t, place], sibling
+        )
+
+    beyond = []
+    if chips > 1:
+        attend(1 - side, False)
+        across = []
+
+        def hand_over(t):
+            across[t].wait_recv()
+            far_send[t] = (gv_mine[t, 1] + gv_recv[t, 1].astype(F32)).astype(BF16)
+            beyond.append(send(far_send.at[t], far_recv.at[t], far_sem.at[t], far_rsem.at[t], mate_device[2]))
+
+        for t in range(tiles):
+            across.append(across_cores(1 - side, 1, t))
+            gv_mine[t, 1] = back(core * chips + 1 - side, t)
+            if t > 0:
+                hand_over(t - 1)
+        hand_over(tiles - 1)
+    attend(side, chips > 1)
     grad_sum = reduce_gather(grads, gstage, ghalves, gfull, g_send, g_recv, finish_grads)
     next(grad_sum)
-    half_rows = chips * toks
-
-    def back(who, t):
-        left = gquery[pl.ds(pl.multiple_of(who * half_rows, half_rows), half_rows), :]
-        return dot(left, wqt[:, t * span : (t + 1) * span], (1, 0)).reshape(chips, toks, span)
-
-    across, beyond = [], []
-
-    def hand_over(t):
-        across[t].wait_recv()
-        if chips > 1:
-            far_send[t] = (gv_mine[t, 1 - side] + gv_recv[t, 1 - side].astype(F32)).astype(BF16)
-            beyond.append(send(far_send.at[t], far_recv.at[t], far_sem.at[t], far_rsem.at[t], mate_device[2]))
-
+    near_copies = []
     for t in range(tiles):
-        gv_send[t] = back(1 - core, t).astype(BF16)
-        across.append(send(gv_send.at[t], gv_recv.at[t], gv_sem.at[t], gv_rsem.at[t], sibling))
-        gv_mine[t] = back(core, t)
+        near_copies.append(across_cores(side, 0, t))
+        gv_mine[t, 0] = back(core * chips + side, t)
         drain(grad_sum, 1)
-        if t > 0:
-            hand_over(t - 1)
-    hand_over(tiles - 1)
     drain(grad_sum)
 
     gk, gv = gfull[0].reshape(text_len, width), gfull[1].reshape(text_len, width)
@@ -422,7 +442,8 @@
     total = dot(gk, wk[member], (1, 1)) + dot(gv, wv[member], (1, 1))
     for t in range(tiles):
         cols = slice(t * span, (t + 1) * span)
-        tile_sum = gv_mine[t, side] + gv_recv[t, side].astype(F32)
+        near_copies[t].wait_recv()
+        tile_sum = gv_mine[t, 0] + gv_recv[t, 0].astype(F32)
         if chips > 1:
             beyond[t].wait_recv()
             tile_sum = tile_sum + far_recv[t].astype(F32)
@@ -518,8 +539,8 @@
             dma((2, 2 * n_bits)),
             dma((2, 2 * n_bits)),
             dma((2, 2 * n_bits)),
-            dma((tiles,)),
-            dma((tiles,)),
+            dma((tiles, 2)),
+            dma((tiles, 2)),
             dma((tiles,)),
             dma((tiles,)),
             dma((2, size)),

time: 247 us -> 246 us (level)
  no operation moved by 1% of the time
where the time goes in v6:
time: 246 us
  Pallas kernels  237 us (96%)
  local copies, waits for them, and re-layouts  4.42 us (2%)
  other arithmetic  3.89 us (2%)
    pallas_call x1, Pallas kernels, body(): pl.pallas_call(functools.partial(kernel, n, size, text_dim), out_shape=[j...  237 us

profile of v6, /device:TPU:4, one launch (start us, length us, event | category | flops | bytes accessed | tf_op | source)
XLA Modules:
  0.0 245.7 jit_solution(7301079545779929632)
XLA Ops:
  0.6 1.5 fusion.1
  2.1 0.8 broadcast_in_dim.2.squares
  2.9 0.0 copy-start
  2.9 0.0 copy-start.1
  2.9 236.7 %shard_map.95 = (bf16[256,3072]{1,0:T(8,128)(2,1)}, f32[256,128]{1,0:T(8,128)}, f32[8,256]{1,0:T(8,128)}, f32[256,128]{1,0:T(8,128)}) custom-call(bf16[256,128]{1,0:T(8,128)(2,1)} %get-tuple-element.11.scaled, f32[256,128]{1,0:T(8,128)} %broadcast_in_dim.2.squares, bf16[128,3072]{1,0:T(8,128)(2,1)} %w_key.1, bf16[128,3072]{1,0:T(8,128)(2,1)} %w_value.1, ...), custom_call_target="tpu_custom_call" | custom-call | flops 16508780544 | bytes 6291456 | tf_op jit(solution)/shard_map/pallas_call | solution.py:487
  239.6 0.7 slice_multiply_fusion
  240.3 1.0 slice_reduce_fusion
  241.3 0.0 copy-done
  241.3 0.0 copy-done.1
  241.3 1.7 fusion.4
  243.0 2.7 %copy.11 = bf16[256,3072]{1,0:T(8,128)(2,1)} copy(bf16[256,3072]{1,0:T(8,128)(2,1)} %get-tuple-element.14) | data formatting | bytes 3145728
Async XLA Ops:
  2.9 238.4 %copy-start = (bf16[256,128]{1,0:T(8,128)(2,1)S(1)}, bf16[256,128]{1,0:T(8,128)(2,1)}, u32[]{:S(2)}) copy-start(bf16[256,128]{1,0:T(8,128)(2,1)} %param.10) | copy-start | bytes 196612
  2.9 238.4 %copy-start.1 = (f32[128]{0:T(128)S(1)}, f32[128]{0:T(128)}, u32[]{:S(2)}) copy-start(f32[128]{0:T(128)} %param.11) | copy-start | bytes 1540
